TPU v7x, 256 devices: a whole 4x4x8 slice. The times are simulated.
256 devices in a mesh: layer: 8 (over z_hi, core), latent: 32 (over x, z_lo, y).
Axes of the slice: x: 4, y: 4, z: 8 (z_hi: 4, z_lo: 2; z = z_hi * 2 + z_lo), core: 2. Of those that a mesh axis runs over, the one named last changes fastest.
Arguments:
- ids: int32 [512], replicated, may hold values from 0 to 511
- bank: bfloat16 [512, 10752], P('latent', 'layer'), may hold values from -6 to 6
- enc_weight: bfloat16 [10752, 32768], P('layer', 'latent'), may hold values from -0.0625 to 0.0625
- enc_bias: float32 [32768], P('latent'), may hold values from -3 to 3
- dec_weight: bfloat16 [32768, 10752], P('latent', 'layer'), may hold values from -0.198873782 to 0.198873782
- dec_bias: float32 [10752], P('layer'), may hold values from -3 to 3
Outputs:
- grad_encoder: bfloat16 [10752, 32768], P('layer', 'latent')
- grad_decoder: bfloat16 [32768, 10752], P('latent', 'layer')
All inputs are finite; a program needn't handle non-finite values.
Results may differ from a plain program's by a relative error of at most 0.025.
Values may be sent and summed in bfloat16 or wider, within the bound.
A program may use at most 64 MiB of HBM per device.

v0:
```python
import math

import jax
import jax.numpy as jnp
from jax import lax
from jax.sharding import PartitionSpec as P

D = 3584
LAYERS = 3


penalty_weight = 0.3


def shards(ids, bank, enc_weight, enc_bias, dec_weight, dec_bias):
    tokens = ids.shape[0]
    feat_dev = bank.shape[1]
    scale = 1.0 / math.sqrt(tokens)
    stored = lax.all_gather(bank, "latent", axis=0, tiled=True)
    inputs = jnp.take(stored, ids, axis=0)
    feature = lax.axis_index("layer") * feat_dev + lax.iota(jnp.int32, feat_dev)
    owner = feature // D
    onehot = (owner[:, None] == lax.iota(jnp.int32, LAYERS)[None, :]).astype(jnp.float32)
    wide = dec_weight.astype(jnp.float32)
    square_part = jnp.dot(wide * wide, onehot, precision=lax.Precision.HIGHEST)
    pre_part = jnp.dot(inputs, enc_weight, preferred_element_type=jnp.float32)
    pre_sum, squares = (
        lax.psum(pre_part.astype(jnp.bfloat16), "layer").astype(jnp.float32),
        lax.psum(square_part.astype(jnp.bfloat16), "layer").astype(jnp.float32),
    )
    pre = pre_sum + enc_bias
    latents = jax.nn.softplus(pre).astype(jnp.bfloat16)
    slope = jax.nn.sigmoid(pre)
    norms = jnp.sqrt(squares + 1e-06)
    total_norm = jnp.sum(norms, axis=1)
    recon_part = jnp.dot(latents, dec_weight, preferred_element_type=jnp.float32)
    recon = lax.psum(recon_part.astype(jnp.bfloat16), "latent").astype(jnp.float32) + dec_bias
    resid_grad = ((recon - inputs.astype(jnp.float32)) * scale).astype(jnp.bfloat16)
    grad_part = lax.dot_general(
        resid_grad, dec_weight, (((1,), (1,)), ((), ())), preferred_element_type=jnp.float32
    )
    latent_grad = lax.psum(grad_part.astype(jnp.bfloat16), "layer").astype(jnp.float32)
    latent_grad = latent_grad + penalty_weight * scale * total_norm[None, :]
    pre_grad = (latent_grad * slope).astype(jnp.bfloat16)
    grad_encoder = lax.dot_general(
        inputs, pre_grad, (((0,), (0,)), ((), ())), preferred_element_type=jnp.float32
    )
    colsum = jnp.sum(latents.astype(jnp.float32), axis=0)
    inverse = jnp.dot(1.0 / norms, onehot.T, precision=lax.Precision.HIGHEST)
    grad_decoder = lax.dot_general(
        latents, resid_grad, (((0,), (0,)), ((), ())), preferred_element_type=jnp.float32
    )
    grad_decoder = grad_decoder + (penalty_weight * scale * colsum)[:, None] * wide * inverse
    return (grad_encoder.astype(jnp.bfloat16), grad_decoder.astype(jnp.bfloat16))


def solution(mesh):
    in_specs = (
        P(),
        P("latent", "layer"),
        P("layer", "latent"),
        P("latent"),
        P("latent", "layer"),
        P("layer"),
    )
    out_specs = (P("layer", "latent"), P("latent", "layer"))
    return jax.shard_map(shards, mesh=mesh, in_specs=in_specs, out_specs=out_specs, check_vma=False)
```

profile of v0, /device:TPU:1, one launch (start us, length us, event | category | flops | bytes accessed | tf_op | source)
XLA Modules:
  0.0 660.8 jit_solution(5217823070440383429)
XLA Ops:
  7.2 0.0 copy-start
  7.2 0.0 all-gather.2.cloned.1.call-start
  7.2 0.7 all-gather.2.cloned.1.call-update
  7.9 0.0 all-reduce.4.cloned.1.call-start
  8.0 0.7 compare_select_fusion.1
  8.7 0.7 compare_and_fusion
  9.4 137.9 %all-gather.2.cloned.1.call-done = bf16[512,1344]{1,0:T(8,128)(2,1)} async-done(((bf16[16,1344]{1,0:T(8,128)(2,1)}), bf16[512,1344]{1,0:T(8,128)(2,1)}) %all-gather.2.cloned.1.call-update) | async-done | bytes 1376272 | tf_op jit(solution)/shard_map/all_gather | solution.py:19
  147.3 5.6 gather_fusion
  152.9 2.5 copy.8
  155.5 0.0 copy-done
  155.5 4.1 convolution_convert_fusion.3
  159.6 0.0 all-reduce.4.cloned.1.call-update
  159.6 0.0 all-reduce.6.cloned.1.call-start
  159.7 96.3 %all-reduce.4.cloned.1.call-done = bf16[512,1024]{1,0:T(8,128)(2,1)} async-done(((bf16[512,1024]{1,0:T(8,128)(2,1)}), bf16[512,1024]{1,0:T(8,128)(2,1)}) %all-reduce.4.cloned.1.call-update) | async-done | bytes 1048592 | tf_op jit(solution)/shard_map/psum | solution.py:28
  256.0 0.0 copy-done.3
  256.0 5.1 convolution_convert_fusion.1
  261.1 0.0 all-reduce.6.cloned.1.call-update
  261.1 0.0 all-reduce.8.cloned.1.call-start
  261.2 0.0 copy-start.2
  261.2 4.0 fusion.5
  265.2 15.8 %psum.31 = bf16[1024,3]{0,1:T(4,128)(2,1)S(1)} all-reduce(bf16[1024,3]{0,1:T(4,128)(2,1)S(1)} %fusion.5), channel_id=1, replica_groups=mesh['layer'=8,'latent'=32] {'layer'}, use_global_device_ids=true, to_apply=%region_3.4 | all-reduce | flops 3072 | bytes 12288 | tf_op jit(solution)/shard_map/psum | solution.py:29
  281.1 2.5 convert_reduce_fusion
  283.6 265.4 %all-reduce.6.cloned.1.call-done = bf16[512,1344]{0,1:T(8,128)(2,1)} async-done(((bf16[512,1344]{0,1:T(8,128)(2,1)}), bf16[512,1344]{0,1:T(8,128)(2,1)}) %all-reduce.6.cloned.1.call-update) | async-done | bytes 1376272 | tf_op jit(solution)/shard_map/psum | solution.py:37
  549.0 0.0 copy-done.2
  549.0 5.5 convolution_convert_fusion.2
  554.6 0.0 all-reduce.8.cloned.1.call-update
  554.6 0.0 copy-start.1
  554.6 4.8 fusion.23
  559.4 0.0 copy-done.1
  559.4 4.5 fusion.3
  563.9 85.1 %all-reduce.8.cloned.1.call-done = bf16[512,1024]{1,0:T(8,128)(2,1)} async-done(((bf16[512,1024]{1,0:T(8,128)(2,1)}), bf16[512,1024]{1,0:T(8,128)(2,1)}) %all-reduce.8.cloned.1.call-update) | async-done | bytes 1048592 | tf_op jit(solution)/shard_map/psum | solution.py:42
  649.0 5.2 convolution_convert_fusion
  (6 shorter events, 0.1 us)
Async XLA Ops:
  7.2 148.3 %copy-start = (bf16[1344,1024]{1,0:T(8,128)(2,1)S(1)}, bf16[1344,1024]{1,0:T(8,128)(2,1)}, u32[]{:S(2)}) copy-start(bf16[1344,1024]{1,0:T(8,128)(2,1)} %param.8) | copy-start | bytes 8257540
  7.2 140.1 %all-gather.2.cloned.1.call-start = ((), (), s32[]{:S(2)}) async-start(), calls=%async_computation | async-start | bytes 1486848 | tf_op jit(solution)/shard_map/all_gather | solution.py:19
  7.9 248.0 %all-reduce.4.cloned.1.call-start = ((), (), s32[]{:S(2)}) async-start(), calls=%async_computation.1 | async-start | bytes 2097152 | tf_op jit(solution)/shard_map/psum | solution.py:28
  155.5 100.5 %copy-start.3 = (f32[1024]{0:T(1024)S(1)}, f32[1024]{0:T(1024)}, u32[]{:S(2)}) copy-start(f32[1024]{0:T(1024)} %param.9) | copy-start | bytes 12292
  159.6 389.4 %all-reduce.6.cloned.1.call-start = ((), (), s32[]{:S(2)}) async-start(), calls=%async_computation.2 | async-start | bytes 2752512 | tf_op jit(solution)/shard_map/psum | solution.py:37
  261.1 387.9 %all-reduce.8.cloned.1.call-start = ((), (), s32[]{:S(2)}) async-start(), calls=%async_computation.3 | async-start | bytes 2097152 | tf_op jit(solution)/shard_map/psum | solution.py:42
  261.2 287.9 %copy-start.2 = (f32[1344]{0:T(1024)S(1)}, f32[1344]{0:T(1024)}, u32[]{:S(2)}) copy-start(f32[1344]{0:T(1024)} %param.11) | copy-start | bytes 16132
  554.6 4.9 copy-start.1
Sparse Core Ops, SparseCore 0:
  9.8 137.4 all-gather.1
  159.8 96.1 all-reduce.3
  261.2 287.8 all-reduce.5
  554.7 94.2 all-reduce.7
where the time goes:
time: 661 us
  waiting for transfers between devices  585 us (89%)
  matrix products  33.3 us (5%)
  blocking collectives  15.8 us (2%)
  between operations  13.9 us (2%)
  local copies, waits for them, and re-layouts  8.2 us (1%)
    psum x1, waiting for transfers between devices, shards(): lax.psum(recon_part.astype(jnp.bfloat16), 'latent').astype(jnp.float32)  265 us
    all_gather x1, waiting for transfers between devices, shards(): stored = lax.all_gather(bank, 'latent', axis=0, tiled=True)  138 us
    psum x1, waiting for transfers between devices, shards(): lax.psum(pre_part.astype(jnp.bfloat16), 'layer').astype(jnp.float32)  96.3 us
    psum x1, waiting for transfers between devices, shards(): lax.psum(grad_part.astype(jnp.bfloat16), 'layer').astype(jnp.float32)  85.1 us
    psum x1, blocking collectives, shards(): lax.psum(square_part.astype(jnp.bfloat16), 'layer').astype(jnp.float32)  15.8 us
  transfers between devices with their start and end apart: 4, of which 4 were waited for; matrix products, arithmetic and copies ran while one was open for 3% of the time, Pallas kernels for 0%

commit v1 on v0

v1 whole, which is shorter than its diff:
```python
import functools
import math

import jax
import jax.numpy as jnp
from jax import lax
from jax.experimental import pallas as pl
from jax.experimental.pallas import tpu as pltpu
from jax.sharding import PartitionSpec as P

D = 3584
LAYERS = 3
PENALTY = 0.3
ROWS = 16
F0 = 640
CHUNKS = 2
MESH = pl.DeviceIdType.MESH
BF = jnp.bfloat16
F32 = jnp.float32


class Links:
    def __init__(self, send_sems, recv_sems, me):
        self.send_sems, self.recv_sems, self.me = send_sems, recv_sems, me
        self.names, self.pending = {}, []

    def number(self, name):
        return self.names.setdefault(name, len(self.names))

    def copy(self, name, src, dst, device):
        i = self.number(name)
        return pltpu.make_async_remote_copy(
            src_ref=src,
            dst_ref=dst,
            send_sem=self.send_sems.at[i],
            recv_sem=self.recv_sems.at[i],
            device_id=device,
            device_id_type=MESH,
        )

    def send(self, name, src, dst, device):
        copy = self.copy(name, src, dst, device)
        copy.start()
        self.pending.append(copy)

    def recv(self, name, view):
        self.copy(name, view, view, self.me).wait_recv()

    def drain(self):
        for copy in self.pending:
            copy.wait_send()
        self.pending = []


class Ring:
    def __init__(self, place, device_at):
        self.place, self.device_at = place, device_at

    def at(self, shift):
        return lax.rem(self.place + shift % 4, 4)

    def device(self, shift):
        return self.device_at(self.at(shift))


def gather_start(links, tag, ring, view):
    p = ring.at(0)
    links.send((tag, "n0"), view(p, 0), view(p, 0), ring.device(1))
    links.send((tag, "p1"), view(p, 1), view(p, 1), ring.device(-1))
    links.send((tag, "n1"), view(p, 1), view(p, 1), ring.device(1))
    links.send((tag, "p0"), view(p, 0), view(p, 0), ring.device(-1))


def gather_forward(links, tag, ring, view):
    left, right = ring.at(-1), ring.at(1)
    links.recv((tag, "n0"), view(left, 0))
    links.send((tag, "fn"), view(left, 0), view(left, 0), ring.device(1))
    links.recv((tag, "p1"), view(right, 1))
    links.send((tag, "fp"), view(right, 1), view(right, 1), ring.device(-1))


def gather_finish(links, tag, ring, view):
    links.recv((tag, "n1"), view(ring.at(-1), 1))
    links.recv((tag, "p0"), view(ring.at(1), 0))
    links.recv((tag, "fn"), view(ring.at(2), 0))
    links.recv((tag, "fp"), view(ring.at(2), 1))


def scatter_start(links, tag, ring, part, got):
    links.send((tag, "f0"), part(ring.at(2), 0), got(0), ring.device(1))
    links.send((tag, "f1"), part(ring.at(2), 1), got(1), ring.device(-1))
    links.send((tag, "d1"), part(ring.at(1), 1), got(2), ring.device(1))
    links.send((tag, "d0"), part(ring.at(-1), 0), got(3), ring.device(-1))


def scatter_middle(links, tag, ring, part, got, both):
    links.recv((tag, "f0"), got(0))
    both(0)[...] = (part(ring.at(1), 0)[...].astype(F32) + got(0)[...].astype(F32)).astype(BF)
    links.send((tag, "c0"), both(0), got(4), ring.device(1))
    links.recv((tag, "f1"), got(1))
    both(1)[...] = (part(ring.at(-1), 1)[...].astype(F32) + got(1)[...].astype(F32)).astype(BF)
    links.send((tag, "c1"), both(1), got(5), ring.device(-1))


def scatter_finish(links, tag, ring, part, got):
    p = ring.at(0)
    links.recv((tag, "d0"), got(3))
    links.recv((tag, "c0"), got(4))
    first = part(p, 0)[...].astype(F32) + got(3)[...].astype(F32) + got(4)[...].astype(F32)
    links.recv((tag, "d1"), got(2))
    links.recv((tag, "c1"), got(5))
    second = part(p, 1)[...].astype(F32) + got(2)[...].astype(F32) + got(5)[...].astype(F32)
    return first, second


def direct_start(links, tag, ring, source, target):
    for d in (1, 2, 3):
        links.send((tag, d), source(ring.at(d)), target(ring.at(0)), ring.device(d))


def direct_finish(links, tag, ring, target):
    for d in (1, 2, 3):
        links.recv((tag, d), target(ring.at(-d)))


def kernel(
    scale,
    ids_ref, bank_ref, bias_ref, dbias_ref, enc_hbm, dec_hbm,
    bank0_out, bank1_out, lat_out, res0_out, res1_out, pg_out, coef_ref,
    enc, dec, blk0, blk1, bk0, bk1,
    parts, from_core, sums, zgot, zboth, lat, pg, slope,
    rp0, rp1, got0, got1, both0, both1, s0, s1, d0, d1, q0, q1, e0, e1, rs0, rs1,
    sq_part, sq_core, sq_chip, sq_z,
    send_sems, recv_sems, local_sems,
):
    layer, latent = lax.axis_index("layer"), lax.axis_index("latent")
    z, core = layer // 2, lax.rem(layer, 2)
    x, y = latent // 8, lax.rem(latent, 4)
    zl = lax.rem(latent // 4, 2)
    features = enc.shape[0]
    ring_z = Ring(z, lambda q: (q * 2 + core, latent))
    ring_x = Ring(x, lambda q: (layer, q * 8 + zl * 4 + y))
    ring_y = Ring(y, lambda q: (layer, x * 8 + zl * 4 + q))
    core_peer = (z * 2 + 1 - core, latent)
    zl_peer = (layer, x * 8 + (1 - zl) * 4 + y)
    links = Links(send_sems, recv_sems, (layer, latent))

    dec_copy = pltpu.make_async_copy(dec_hbm, dec, local_sems.at[0])
    enc_copy = pltpu.make_async_copy(enc_hbm, enc, local_sems.at[1])
    dec_copy.start()
    enc_copy.start()

    partners = [core_peer, zl_peer]
    for ring in (ring_x, ring_y, ring_z):
        partners += [ring.device(d) for d in (1, 2, 3)]
    barrier = pltpu.get_barrier_semaphore()
    for device in partners:
        pl.semaphore_signal(barrier, inc=1, device_id=device, device_id_type=MESH)
    pl.semaphore_wait(barrier, len(partners))

    def counts(rows):
        hits = (ids_ref[...] == rows).astype(F32)
        return jnp.sum(hits, axis=1, keepdims=True)

    def bank_rows(k, block, n):
        i = lax.broadcasted_iota(jnp.int32, (n, 1), 0)
        b = block + i // ROWS
        return ((b // 4 * 2 + k) * 4 + lax.rem(b, 4)) * ROWS + lax.rem(i, ROWS)

    def x_view(buf, k):
        return lambda q, h: buf.at[k, q, pl.ds(2 * h, 2)]

    def y_view(buf, k):
        return lambda q, h: buf.at[k, pl.ds(2 * h, 2), q]

    def plane_first_start(tag, k, b0, b1):
        direct_start(links, (tag, k, 0), ring_y, lambda q: b0.at[k, x, y], lambda q: b0.at[k, x, q])
        direct_start(links, (tag, k, 1), ring_x, lambda q: b1.at[k, x, y], lambda q: b1.at[k, q, y])

    def plane_first_finish(tag, k, b0, b1):
        direct_finish(links, (tag, k, 0), ring_y, lambda q: b0.at[k, x, q])
        direct_finish(links, (tag, k, 1), ring_x, lambda q: b1.at[k, q, y])

    def plane_second(step, tag, k, b0, b1):
        step(links, (tag, k, "x"), ring_x, x_view(b0, k))
        step(links, (tag, k, "y"), ring_y, y_view(b1, k))

    def z_part(s, k):
        return lambda q, h: sums.at[s, k, q, h]

    def z_got(s, k):
        return lambda i: zgot.at[s, k, i]

    def z_both(s, k):
        return lambda i: zboth.at[s, k, i]

    def z_view(buf, k):
        return lambda q, h: buf.at[k, core, q, h]

    def product_send(s, k):
        links.send(("core", s, k), parts.at[s, k, 1 - core], from_core.at[s, k], core_peer)

    def z_scatter_start(s, k):
        links.recv(("core", s, k), from_core.at[s, k])
        own = parts[s, k, core].astype(F32) + from_core[s, k].astype(F32)
        sums[s, k] = own.astype(BF)
        scatter_start(links, ("zs", s, k), ring_z, z_part(s, k), z_got(s, k))

    def z_scatter_middle(s, k):
        scatter_middle(links, ("zs", s, k), ring_z, z_part(s, k), z_got(s, k), z_both(s, k))

    def z_scatter_finish(s, k):
        return scatter_finish(links, ("zs", s, k), ring_z, z_part(s, k), z_got(s, k))

    def z_gather_start(s, k, buf):
        gather_start(links, ("zg", s, k), ring_z, z_view(buf, k))
        own = buf.at[k, core, z]
        links.send(("zc", s, k, 0), own, own, core_peer)

    def z_gather_forward(s, k, buf):
        gather_forward(links, ("zg", s, k), ring_z, z_view(buf, k))

    def z_gather_finish(s, k, buf):
        view = z_view(buf, k)
        links.recv((("zg", s, k), "n1"), view(ring_z.at(-1), 1))
        block = buf.at[k, core, ring_z.at(-1)]
        links.send(("zc", s, k, 1), block, block, core_peer)
        links.recv((("zg", s, k), "p0"), view(ring_z.at(1), 0))
        block = buf.at[k, core, ring_z.at(1)]
        links.send(("zc", s, k, 2), block, block, core_peer)
        links.recv((("zg", s, k), "fn"), view(ring_z.at(2), 0))
        links.recv((("zg", s, k), "fp"), view(ring_z.at(2), 1))
        block = buf.at[k, core, ring_z.at(2)]
        links.send(("zc", s, k, 3), block, block, core_peer)
        for i, shift in enumerate((0, -1, 1, 2)):
            links.recv(("zc", s, k, i), buf.at[k, 1 - core, ring_z.at(shift)])

    def encode(k):
        b0 = bk0[k].reshape(256, F0)
        b1 = bk1[k].reshape(256, features - F0)

        def tile(n, carry):
            at = pl.ds(pl.multiple_of(n * 256, 256), 256)
            out = jnp.dot(b0, enc[:F0, at], preferred_element_type=F32)
            out += jnp.dot(b1, enc[F0:, at], preferred_element_type=F32)
            parts[0, k, :, :, :, :, at] = out.astype(BF).reshape(2, 4, 2, ROWS, 256)
            return carry

        lax.fori_loop(0, 4, tile, 0)
        product_send(0, k)

    def latents(k):
        halves = z_scatter_finish(0, k)
        for h in (0, 1):
            pre = halves[h] + bias_ref[...]
            soft = jnp.maximum(pre, 0.0) + jnp.log1p(jnp.exp(-jnp.abs(pre)))
            lat[k, core, z, h] = soft.astype(BF)
            slope[k, h] = jax.nn.sigmoid(pre)
        z_gather_start(0, k, lat)

    def decode(k):
        rows = lat[k].reshape(256, 1024)
        out = jnp.dot(rows, dec[:, :F0], preferred_element_type=F32)
        rp0[k] = out.astype(BF).reshape(4, 4, ROWS, F0)
        scatter_start(links, ("xs", k), ring_x, x_view(rp0, k), lambda i: got0.at[k, i])
        out = jnp.dot(rows, dec[:, F0:], preferred_element_type=F32)
        rp1[k] = out.astype(BF).reshape(4, 4, ROWS, features - F0)
        scatter_start(links, ("ys", k), ring_y, y_view(rp1, k), lambda i: got1.at[k, i])

    def recon_middle(k):
        scatter_middle(
            links, ("xs", k), ring_x, x_view(rp0, k), lambda i: got0.at[k, i], lambda i: both0.at[k, i]
        )
        scatter_middle(
            links, ("ys", k), ring_y, y_view(rp1, k), lambda i: got1.at[k, i], lambda i: both1.at[k, i]
        )

    def recon_second(k):
        a, b = scatter_finish(links, ("xs", k), ring_x, x_view(rp0, k), lambda i: got0.at[k, i])
        s0[k, 0:2] = a.astype(BF)
        s0[k, 2:4] = b.astype(BF)
        direct_start(links, ("xt", k), ring_y, lambda q: s0.at[k, q], lambda q: d0.at[k, q])
        a, b = scatter_finish(links, ("ys", k), ring_y, y_view(rp1, k), lambda i: got1.at[k, i])
        s1[k, 0:2] = a.astype(BF)
        s1[k, 2:4] = b.astype(BF)
        direct_start(links, ("yt", k), ring_x, lambda q: s1.at[k, q], lambda q: d1.at[k, q])

    def recon_third(k):
        for tag, ring, s, d, q, e in (("xt", ring_y, s0, d0, q0, e0), ("yt", ring_x, s1, d1, q1, e1)):
            direct_finish(links, (tag, k), ring, lambda j: d.at[k, j])
            total = s[k, ring.at(0)].astype(F32)
            for shift in (1, 2, 3):
                total += d[k, ring.at(shift)].astype(F32)
            q[k] = total.astype(BF)
            links.send((tag, "zl", k), q.at[k], e.at[k], zl_peer)

    def residual(k, own_counts):
        for tag, at, q, e, bk, rs in (
            ("xt", pl.ds(0, F0), q0, e0, bk0, rs0),
            ("yt", pl.ds(F0, features - F0), q1, e1, bk1, rs1),
        ):
            links.recv((tag, "zl", k), e.at[k])
            recon = q[k].astype(F32) + e[k].astype(F32) + dbias_ref[:, at]
            value = (recon - bk[k, x, y].astype(F32)) * scale
            rs[k, x, y] = (value * own_counts).astype(BF)
        plane_first_start("r", k, rs0, rs1)

    def backward(k):
        r0 = rs0[k].reshape(256, F0)
        r1 = rs1[k].reshape(256, features - F0)
        over = (((1,), (1,)), ((), ()))

        def tile(n, carry):
            at = pl.ds(pl.multiple_of(n * 256, 256), 256)
            out = lax.dot_general(r0, dec[at, :F0], over, preferred_element_type=F32)
            out += lax.dot_general(r1, dec[at, F0:], over, preferred_element_type=F32)
            parts[1, k, :, :, :, :, at] = out.astype(BF).reshape(2, 4, 2, ROWS, 256)
            return carry

        lax.fori_loop(0, 4, tile, 0)
        product_send(1, k)

    def latent_gradient(k, row_counts, total_norm):
        halves = z_scatter_finish(1, k)
        for h in (0, 1):
            weight = row_counts[h * ROWS : (h + 1) * ROWS]
            grad = halves[h] + weight * (PENALTY * scale * total_norm)
            pg[k, core, z, h] = (grad * slope[k, h]).astype(BF)
        z_gather_start(1, k, pg)

    blk0[zl] = bank_ref[:, :F0]
    blk1[zl] = bank_ref[:, F0:]
    links.send("bz0", blk0.at[zl], blk0.at[zl], zl_peer)
    links.send("bz1", blk1.at[zl], blk1.at[zl], zl_peer)
    own_counts = [counts(bank_rows(k, x * 4 + y, ROWS)) for k in range(CHUNKS)]
    row_counts = [counts(bank_rows(k, core * 8 + z * 2, 2 * ROWS)) for k in range(CHUNKS)]
    links.recv("bz0", blk0.at[1 - zl])
    links.recv("bz1", blk1.at[1 - zl])
    for k in range(CHUNKS):
        bk0[k, x, y] = blk0[k]
        bk1[k, x, y] = blk1[k]
        plane_first_start("b", k, bk0, bk1)

    dec_copy.wait()
    row = lax.broadcasted_iota(jnp.int32, (8, features), 0)
    column = lax.broadcasted_iota(jnp.int32, (8, features), 1) + layer * features
    owner = jnp.where((column >= row * D) & (column < (row + 1) * D), 1.0, 0.0).astype(BF)

    def square(n, carry):
        at = pl.ds(pl.multiple_of(n * 256, 256), 256)
        wide = dec[at, :].astype(F32)
        wide = wide * wide
        high = wide.astype(BF)
        low = (wide - high.astype(F32)).astype(BF)
        over = (((1,), (1,)), ((), ()))
        total = lax.dot_general(owner, high, over, preferred_element_type=F32)
        total += lax.dot_general(owner, low, over, preferred_element_type=F32)
        sq_part[:, at] = total
        return carry

    lax.fori_loop(0, 4, square, 0)
    links.send("sqc", sq_part, sq_core, core_peer)

    plane_first_finish("b", 0, bk0, bk1)
    plane_second(gather_start, "b2", 0, bk0, bk1)
    links.recv("sqc", sq_core)
    sq_chip[...] = sq_part[...] + sq_core[...]
    direct_start(links, "sqz", ring_z, lambda q: sq_chip, lambda q: sq_z.at[q])
    plane_first_finish("b", 1, bk0, bk1)
    enc_copy.wait()
    plane_second(gather_forward, "b2", 0, bk0, bk1)
    plane_second(gather_start, "b2", 1, bk0, bk1)
    plane_second(gather_finish, "b2", 0, bk0, bk1)
    encode(0)
    plane_second(gather_forward, "b2", 1, bk0, bk1)
    z_scatter_start(0, 0)
    plane_second(gather_finish, "b2", 1, bk0, bk1)
    encode(1)
    z_scatter_middle(0, 0)
    z_scatter_start(0, 1)
    bank0_copy = pltpu.make_async_copy(bk0, bank0_out, local_sems.at[2])
    bank1_copy = pltpu.make_async_copy(bk1, bank1_out, local_sems.at[3])
    bank0_copy.start()
    bank1_copy.start()
    direct_finish(links, "sqz", ring_z, lambda q: sq_z.at[q])
    squares = sq_chip[...]
    for shift in (1, 2, 3):
        squares += sq_z[ring_z.at(shift)]
    norms = jnp.sqrt(squares + 1e-6)
    total_norm = norms[0:1] + norms[1:2] + norms[2:3]
    latents(0)
    z_scatter_middle(0, 1)
    z_gather_forward(0, 0, lat)
    latents(1)
    z_gather_finish(0, 0, lat)
    decode(0)
    z_gather_forward(0, 1, lat)
    recon_middle(0)
    z_gather_finish(0, 1, lat)
    decode(1)
    recon_second(0)
    recon_middle(1)
    recon_third(0)
    lat_copy = pltpu.make_async_copy(lat, lat_out, local_sems.at[4])
    lat_copy.start()
    recon_second(1)
    residual(0, own_counts[0])
    recon_third(1)
    plane_first_finish("r", 0, rs0, rs1)
    plane_second(gather_start, "r2", 0, rs0, rs1)
    residual(1, own_counts[1])
    plane_second(gather_forward, "r2", 0, rs0, rs1)
    plane_first_finish("r", 1, rs0, rs1)
    plane_second(gather_start, "r2", 1, rs0, rs1)
    plane_second(gather_finish, "r2", 0, rs0, rs1)
    backward(0)
    plane_second(gather_forward, "r2", 1, rs0, rs1)
    z_scatter_start(1, 0)
    plane_second(gather_finish, "r2", 1, rs0, rs1)
    backward(1)
    z_scatter_middle(1, 0)
    z_scatter_start(1, 1)
    res0_copy = pltpu.make_async_copy(rs0, res0_out, local_sems.at[5])
    res1_copy = pltpu.make_async_copy(rs1, res1_out, local_sems.at[6])
    res0_copy.start()
    res1_copy.start()
    latent_gradient(0, row_counts[0], total_norm)
    z_scatter_middle(1, 1)
    z_gather_forward(1, 0, pg)
    latent_gradient(1, row_counts[1], total_norm)
    colsum = jnp.zeros((1, 1024), F32)
    for k in range(CHUNKS):
        weight = counts(bank_rows(k, 0, 256))
        colsum += jnp.sum(lat[k].reshape(256, 1024).astype(F32) * weight, axis=0, keepdims=True)
    coef_ref[...] = (PENALTY * scale * colsum) / norms
    z_gather_finish(1, 0, pg)
    z_gather_forward(1, 1, pg)
    z_gather_finish(1, 1, pg)
    pg_copy = pltpu.make_async_copy(pg, pg_out, local_sems.at[7])
    pg_copy.start()
    links.drain()
    for copy in (bank0_copy, bank1_copy, lat_copy, res0_copy, res1_copy, pg_copy):
        copy.wait()


def shards(ids, bank, enc_weight, enc_bias, dec_weight, dec_bias):
    tokens = ids.shape[0]
    features, lats = enc_weight.shape
    f1 = features - F0
    scale = 1.0 / math.sqrt(tokens)
    k = CHUNKS
    vmem = pl.BlockSpec(memory_space=pltpu.VMEM)
    hbm = pl.BlockSpec(memory_space=pl.ANY)
    messages = 256
    bank0, bank1, lat, res0, res1, pg, coef = pl.pallas_call(
        functools.partial(kernel, scale),
        out_shape=[
            jax.ShapeDtypeStruct((k, 4, 4, ROWS, F0), BF),
            jax.ShapeDtypeStruct((k, 4, 4, ROWS, f1), BF),
            jax.ShapeDtypeStruct((k, 2, 4, 2, ROWS, lats), BF),
            jax.ShapeDtypeStruct((k, 4, 4, ROWS, F0), BF),
            jax.ShapeDtypeStruct((k, 4, 4, ROWS, f1), BF),
            jax.ShapeDtypeStruct((k, 2, 4, 2, ROWS, lats), BF),
            jax.ShapeDtypeStruct((8, lats), F32),
        ],
        in_specs=[vmem, vmem, vmem, vmem, hbm, hbm],
        out_specs=[hbm] * 6 + [vmem],
        scratch_shapes=[
            pltpu.VMEM((features, lats), BF),
            pltpu.VMEM((lats, features), BF),
            pltpu.VMEM((2, ROWS, F0), BF),
            pltpu.VMEM((2, ROWS, f1), BF),
            pltpu.VMEM((k, 4, 4, ROWS, F0), BF),
            pltpu.VMEM((k, 4, 4, ROWS, f1), BF),
            pltpu.VMEM((2, k, 2, 4, 2, ROWS, lats), BF),
            pltpu.VMEM((2, k, 4, 2, ROWS, lats), BF),
            pltpu.VMEM((2, k, 4, 2, ROWS, lats), BF),
            pltpu.VMEM((2, k, 6, ROWS, lats), BF),
            pltpu.VMEM((2, k, 2, ROWS, lats), BF),
            pltpu.VMEM((k, 2, 4, 2, ROWS, lats), BF),
            pltpu.VMEM((k, 2, 4, 2, ROWS, lats), BF),
            pltpu.VMEM((k, 2, ROWS, lats), F32),
            pltpu.VMEM((k, 4, 4, ROWS, F0), BF),
            pltpu.VMEM((k, 4, 4, ROWS, f1), BF),
            pltpu.VMEM((k, 6, 2, ROWS, F0), BF),
            pltpu.VMEM((k, 6, 2, ROWS, f1), BF),
            pltpu.VMEM((k, 2, 2, ROWS, F0), BF),
            pltpu.VMEM((k, 2, 2, ROWS, f1), BF),
            pltpu.VMEM((k, 4, ROWS, F0), BF),
            pltpu.VMEM((k, 4, ROWS, f1), BF),
            pltpu.VMEM((k, 4, ROWS, F0), BF),
            pltpu.VMEM((k, 4, ROWS, f1), BF),
            pltpu.VMEM((k, ROWS, F0), BF),
            pltpu.VMEM((k, ROWS, f1), BF),
            pltpu.VMEM((k, ROWS, F0), BF),
            pltpu.VMEM((k, ROWS, f1), BF),
            pltpu.VMEM((k, 4, 4, ROWS, F0), BF),
            pltpu.VMEM((k, 4, 4, ROWS, f1), BF),
            pltpu.VMEM((8, lats), F32),
            pltpu.VMEM((8, lats), F32),
            pltpu.VMEM((8, lats), F32),
            pltpu.VMEM((4, 8, lats), F32),
            pltpu.SemaphoreType.DMA((messages,)),
            pltpu.SemaphoreType.DMA((messages,)),
            pltpu.SemaphoreType.DMA((8,)),
        ],
        compiler_params=pltpu.CompilerParams(
            collective_id=0, has_side_effects=True, vmem_limit_bytes=56 * 2**20
        ),
        name="crosscoder_step",
    )(ids[None, :], bank, enc_bias[None, :], dec_bias[None, :], enc_weight, dec_weight)

    inputs = jnp.concatenate([bank0.reshape(-1, F0), bank1.reshape(-1, f1)], axis=1)
    resid = jnp.concatenate([res0.reshape(-1, F0), res1.reshape(-1, f1)], axis=1)
    over = (((0,), (0,)), ((), ()))
    grad_encoder = lax.dot_general(inputs, pg.reshape(-1, lats), over, preferred_element_type=F32)
    grad_decoder = lax.dot_general(lat.reshape(-1, lats), resid, over, preferred_element_type=F32)
    feature = lax.axis_index("layer") * features + lax.iota(jnp.int32, features)
    owner = (feature // D)[None, :]
    factor = coef.T
    spread = jnp.where(owner == 0, factor[:, 0:1], jnp.where(owner == 1, factor[:, 1:2], factor[:, 2:3]))
    grad_decoder = grad_decoder + spread * dec_weight.astype(F32)
    return (grad_encoder.astype(BF), grad_decoder.astype(BF))


def solution(mesh):
    in_specs = (
        P(),
        P("latent", "layer"),
        P("layer", "latent"),
        P("latent"),
        P("latent", "layer"),
        P("layer"),
    )
    out_specs = (P("layer", "latent"), P("latent", "layer"))
    return jax.shard_map(shards, mesh=mesh, in_specs=in_specs, out_specs=out_specs, check_vma=False)
```

time: 661 us -> 129 us (0.20)
  waiting for transfers between devices: 585 us -> 0 us
  Pallas kernels: 0 us -> 112 us
  matrix products: 33.3 us -> 8.72 us
  blocking collectives: 15.8 us -> 0 us
  between operations: 13.9 us -> 0.69 us
    psum x3 -> x0, waiting for transfers between devices: 447 us -> none  [the longest x1 265 us: shards(): lax.psum(recon_part.astype(jnp.bfloat16), 'latent').astype(jnp.float32)]
    all_gather x1 -> x0, waiting for transfers between devices: 138 us -> none  [shards(): stored = lax.all_gather(bank, 'latent', axis=0, tiled=True)]
    pallas_call x0 -> x1, Pallas kernels: none -> 112 us  [shards(): pl.pallas_call(functools.partial(kernel, scale), out_shape=[jax.ShapeDtyp...]
    dot_general x7 -> x2, matrix products: 33.3 us -> 8.72 us  [the longest x1 5.54 us: shards(): lax.dot_general(lat.reshape(-1, lats), resid, over, preferred_element_typ...]
    psum x1 -> x0, blocking collectives: 15.8 us -> none  [shards(): lax.psum(square_part.astype(jnp.bfloat16), 'layer').astype(jnp.float32)]
    gather x2 -> x0, local copies, waits for them, and re-layouts: 8.18 us -> none  [shards(): inputs = jnp.take(stored, ids, axis=0)]
  transfers between devices with their start and end apart: 4 -> 0, of which waited for: 4 -> 0; matrix products, arithmetic and copies ran while one was open for 3% -> 0% of each run, Pallas kernels for 0% -> 0%
where the time goes in v1:
time: 129 us; the launch traced here: 128 us
  Pallas kernels  112 us (87%)
  matrix products  8.72 us (7%)
  local copies, waits for them, and re-layouts  6.71 us (5%)
    pallas_call x1, Pallas kernels, shards(): pl.pallas_call(functools.partial(kernel, scale), out_shape=[jax.ShapeDtyp...  112 us
    dot_general x1, matrix products, shards(): lax.dot_general(lat.reshape(-1, lats), resid, over, preferred_element_typ...  5.54 us
    unnamed x9, local copies, waits for them, and re-layouts  4.54 us
    dot_general x1, matrix products, shards(): lax.dot_general(inputs, pg.reshape(-1, lats), over, preferred_element_typ...  3.18 us

profile of v1, /device:TPU:1, one launch (start us, length us, event | category | flops | bytes accessed | tf_op | source)
XLA Modules:
  0.0 128.3 jit_solution(621323547137134342)
XLA Ops:
  0.7 1.3 %broadcast_in_dim.58.dbias_ref = f32[1,1344]{1,0:T(1,128)} reshape(f32[1344]{0:T(1024)} %param.11) | data formatting | bytes 10752 | tf_op jit(solution)/shard_map/broadcast_in_dim | solution.py:511
  2.0 4.5 %copy.8.dec_hbm = bf16[1024,1344]{1,0:T(8,128)(2,1)} copy(bf16[1024,1344]{0,1:T(8,128)(2,1)} %param.10) | data formatting | bytes 5505024 | tf_op args[4]
  6.5 0.0 copy-start
  6.5 112.2 %crosscoder_step.1 = (bf16[2,4,4,16,640]{4,3,2,1,0:T(8,128)(2,1)}, bf16[2,4,4,16,704]{4,3,2,1,0:T(8,128)(2,1)}, bf16[2,2,4,2,16,1024]{5,4,3,2,1,0:T(8,128)(2,1)}...) custom-call(s32[1,512]{1,0:T(1,128)} %bitcast.19, ...), custom_call_target="tpu_custom_call" | custom-call | tf_op jit(solution)/shard_map/crosscoder_step/pallas_call | solution.py:455
  118.7 0.9 fusion.9
  119.6 0.0 copy-done
  119.6 0.0 copy-start.1
  119.6 0.0 copy-start.2
  119.6 0.0 copy-start.3
  119.6 5.5 %add_convert_fusion = bf16[1024,1344]{0,1:T(8,128)(2,1)} fusion(bf16[1024,1344]{0,1:T(8,128)(2,1)S(1)} %copy-done, bf16[512,1024]{1,0:T(8,128)(2,1)} %bitcast.21, f32[1024]{0:T(1024)S(1)} %bitcast.16, f32[1024]{0:T(1024)S(1)} %bitcast.17, f32[1024]{0:T(1024)S(1)} %bitcast.15, pred[1344]{0:T(1024)(128)(4,1)S(1)} %get-tuple-element.20, ...), kind=kOutput, calls=%fused_computation | convolution fusion | flops 1420296192 | bytes 7944832 | tf_op jit(solution)/shard_map/dot_general | solution.py:517
  125.2 0.0 copy-done.1
  125.2 0.0 copy-done.2
  125.2 0.0 copy-done.3
  125.2 3.2 %convolution_convert_fusion = bf16[1344,1024]{1,0:T(8,128)(2,1)} fusion(bf16[512,1024]{1,0:T(8,128)(2,1)S(1)} %bitcast.20, bf16[512,704]{1,0:T(8,128)(2,1)S(1)} %bitcast.22, bf16[512,640]{1,0:T(8,128)(2,1)S(1)} %bitcast.24), kind=kOutput, calls=%fused_computation.1 | convolution fusion | flops 1413414912 | bytes 5177344 | tf_op jit(solution)/shard_map/dot_general | solution.py:516
  (1 shorter events, 0.0 us)
Async XLA Ops:
  6.5 113.1 %copy-start = (bf16[1024,1344]{0,1:T(8,128)(2,1)S(1)}, bf16[1024,1344]{0,1:T(8,128)(2,1)}, u32[]{:S(2)}) copy-start(bf16[1024,1344]{0,1:T(8,128)(2,1)} %param.10) | copy-start | bytes 8257540
  119.6 5.6 %copy-start.1 = (bf16[2,2,4,2,16,1024]{5,4,3,2,1,0:T(8,128)(2,1)S(1)}, bf16[2,2,4,2,16,1024]{5,4,3,2,1,0:T(8,128)(2,1)}, u32[]{:S(2)}) copy-start(bf16[2,2,4,2,16,1024]{5,4,3,2,1,0:T(8,128)(2,1)} %get-tuple-element.11) | copy-start | bytes 3145732
  119.6 5.6 %copy-start.2 = (bf16[2,4,4,16,704]{4,3,2,1,0:T(8,128)(2,1)S(1)}, bf16[2,4,4,16,704]{4,3,2,1,0:T(8,128)(2,1)}, u32[]{:S(2)}) copy-start(bf16[2,4,4,16,704]{4,3,2,1,0:T(8,128)(2,1)} %get-tuple-element.10) | copy-start | bytes 2162692
  119.6 5.6 %copy-start.3 = (bf16[2,4,4,16,640]{4,3,2,1,0:T(8,128)(2,1)S(1)}, bf16[2,4,4,16,640]{4,3,2,1,0:T(8,128)(2,1)}, u32[]{:S(2)}) copy-start(bf16[2,4,4,16,640]{4,3,2,1,0:T(8,128)(2,1)} %get-tuple-element.9) | copy-start | bytes 1966084

commit v2 on v1

v2 whole, which is shorter than its diff:
```python
import functools
import math

import jax
import jax.numpy as jnp
from jax import lax
from jax.experimental import pallas as pl
from jax.experimental.pallas import tpu as pltpu
from jax.sharding import PartitionSpec as P

D = 3584
LAYERS = 3
PENALTY = 0.3
ROWS = 16
F0 = 640
CHUNKS = 2
MESH = pl.DeviceIdType.MESH
BF = jnp.bfloat16
F32 = jnp.float32


class Links:
    def __init__(self, send_sems, recv_sems, me):
        self.send_sems, self.recv_sems, self.me = send_sems, recv_sems, me
        self.names, self.families = {}, {}

    def copy(self, name, src, dst, device):
        i = self.names.setdefault(name, len(self.names))
        j = self.families.setdefault(name[0], len(self.families))
        return pltpu.make_async_remote_copy(
            src_ref=src,
            dst_ref=dst,
            send_sem=self.send_sems.at[j],
            recv_sem=self.recv_sems.at[i],
            device_id=device,
            device_id_type=MESH,
        )

    def send(self, name, src, dst, device):
        self.copy(name, src, dst, device).start()

    def recv(self, name, view):
        self.copy(name, view, view, self.me).wait_recv()

    def sent(self, family, view):
        i = self.families[family]
        pltpu.make_async_copy(view, view, self.send_sems.at[i]).wait()


class Ring:
    def __init__(self, place, device_at):
        self.place, self.device_at = place, device_at

    def at(self, shift):
        return lax.rem(self.place + shift % 4, 4)

    def device(self, shift):
        return self.device_at(self.at(shift))


def gather_start(links, tag, ring, view):
    p = ring.at(0)
    links.send((*tag, "n0"), view(p, 0), view(p, 0), ring.device(1))
    links.send((*tag, "p1"), view(p, 1), view(p, 1), ring.device(-1))
    links.send((*tag, "own"), view(p, 1), view(p, 1), ring.device(1))
    links.send((*tag, "own"), view(p, 0), view(p, 0), ring.device(-1))


def gather_forward(links, tag, ring, view):
    left, right = ring.at(-1), ring.at(1)
    links.recv((*tag, "n0"), view(left, 0))
    links.send((*tag, "far"), view(left, 0), view(left, 0), ring.device(1))
    links.recv((*tag, "p1"), view(right, 1))
    links.send((*tag, "far"), view(right, 1), view(right, 1), ring.device(-1))


def scatter_start(links, tag, ring, part, got):
    links.send((*tag, "f0"), part(ring.at(2), 0), got(0), ring.device(1))
    links.send((*tag, "f1"), part(ring.at(2), 1), got(1), ring.device(-1))
    links.send((*tag, "end"), part(ring.at(1), 1), got(2), ring.device(1))
    links.send((*tag, "end"), part(ring.at(-1), 0), got(3), ring.device(-1))


def scatter_middle(links, tag, ring, part, got, both):
    links.recv((*tag, "f0"), got(0))
    both(0)[...] = (part(ring.at(1), 0)[...].astype(F32) + got(0)[...].astype(F32)).astype(BF)
    links.send((*tag, "end"), both(0), got(4), ring.device(1))
    links.recv((*tag, "f1"), got(1))
    both(1)[...] = (part(ring.at(-1), 1)[...].astype(F32) + got(1)[...].astype(F32)).astype(BF)
    links.send((*tag, "end"), both(1), got(5), ring.device(-1))


def scatter_finish(links, tag, ring, part, got, last_four):
    p = ring.at(0)
    links.recv((*tag, "end"), last_four)
    first = part(p, 0)[...].astype(F32) + got(3)[...].astype(F32) + got(4)[...].astype(F32)
    second = part(p, 1)[...].astype(F32) + got(2)[...].astype(F32) + got(5)[...].astype(F32)
    return first, second


def direct_start(links, tag, ring, source, target):
    for d in (2, 1, 3):
        links.send(tag, source(ring.at(d)), target(ring.at(0)), ring.device(d))


def kernel(
    scale,
    ids_ref, bank_ref, bias_ref, dbias_ref, enc_hbm, dec_hbm,
    bank0_out, bank1_out, lat_out, res0_out, res1_out, pg_out, coef_ref,
    enc, dec, blk0, blk1, bk0, bk1,
    parts, from_core, sums, zgot, zboth, lat, pg, slope,
    rp0, rp1, got0, got1, s0, s1, d0, d1, q0, q1, e0, e1, rs0, rs1,
    sq_part, sq_core, sq_chip, sq_z, norms_ref,
    send_sems, recv_sems, local_sems,
):
    layer, latent = lax.axis_index("layer"), lax.axis_index("latent")
    z, core = layer // 2, lax.rem(layer, 2)
    x, y = latent // 8, lax.rem(latent, 4)
    zl = lax.rem(latent // 4, 2)
    features = enc.shape[0]
    ring_z = Ring(z, lambda q: (q * 2 + core, latent))
    ring_x = Ring(x, lambda q: (layer, q * 8 + zl * 4 + y))
    ring_y = Ring(y, lambda q: (layer, x * 8 + zl * 4 + q))
    core_peer = (z * 2 + 1 - core, latent)
    zl_peer = (layer, x * 8 + (1 - zl) * 4 + y)
    links = Links(send_sems, recv_sems, (layer, latent))

    dec_copy = pltpu.make_async_copy(dec_hbm, dec, local_sems.at[0])
    enc_copy = pltpu.make_async_copy(enc_hbm, enc, local_sems.at[1])
    dec_copy.start()
    enc_copy.start()

    partners = [core_peer, zl_peer]
    for ring in (ring_x, ring_y, ring_z):
        partners += [ring.device(d) for d in (1, 2, 3)]
    barrier = pltpu.get_barrier_semaphore()
    for device in partners:
        pl.semaphore_signal(barrier, inc=1, device_id=device, device_id_type=MESH)
    pl.semaphore_wait(barrier, len(partners))

    def counts(rows):
        hits = (ids_ref[...][None, :] == rows).astype(F32)
        return jnp.sum(hits, axis=1, keepdims=True)

    def bank_rows(k, block, n):
        i = lax.broadcasted_iota(jnp.int32, (n, 1), 0)
        b = block + i // ROWS
        return ((b // 4 * 2 + k) * 4 + lax.rem(b, 4)) * ROWS + lax.rem(i, ROWS)

    def plane_first_start(tag, k, b0, b1):
        own = b0.at[k, x, y]
        direct_start(links, (tag + "0", k), ring_y, lambda q: own, lambda q: b0.at[k, x, q])
        own = b1.at[k, x, y]
        direct_start(links, (tag + "1", k), ring_x, lambda q: own, lambda q: b1.at[k, q, y])

    def plane_second_start(tag, k, b0, b1):
        links.recv((tag + "0", k), b0.at[k, x, pl.ds(0, 3)])
        own = b0.at[k, x]
        direct_start(links, (tag + "2", k), ring_x, lambda q: own, lambda q: b0.at[k, q])
        links.recv((tag + "1", k), b1.at[k, pl.ds(0, 3), y])
        block = b1.at[k, :, y]
        direct_start(links, (tag + "3", k), ring_y, lambda q: block, lambda q: b1.at[k, :, q])

    def plane_finish(tag, k, b0, b1):
        links.recv((tag + "2", k), b0.at[k, pl.ds(0, 3)])
        links.recv((tag + "3", k), b1.at[k, pl.ds(0, 3)])

    def z_part(s, k):
        return lambda q, h: sums.at[s, k, q, h]

    def z_got(s, k):
        return lambda i: zgot.at[s, k, i]

    def z_both(s, k):
        return lambda i: zboth.at[s, k, i]

    def z_view(buf, k):
        return lambda q, h: buf.at[k, core, q, h]

    def product_send(s, k):
        links.send(("core", s, k), parts.at[s, k, 1 - core], from_core.at[s, k], core_peer)

    def z_scatter_start(s, k):
        links.recv(("core", s, k), from_core.at[s, k])
        own = parts[s, k, core].astype(F32) + from_core[s, k].astype(F32)
        sums[s, k] = own.astype(BF)
        scatter_start(links, ("zs", s, k), ring_z, z_part(s, k), z_got(s, k))

    def z_scatter_middle(s, k):
        scatter_middle(links, ("zs", s, k), ring_z, z_part(s, k), z_got(s, k), z_both(s, k))

    def z_scatter_finish(s, k):
        last_four = zgot.at[s, k, pl.ds(2, 4)]
        return scatter_finish(links, ("zs", s, k), ring_z, z_part(s, k), z_got(s, k), last_four)

    def to_core(s, k, buf, shift):
        block = buf.at[k, core, ring_z.at(shift)]
        links.send(("zc", s, k), block, block, core_peer)

    def z_gather_start(s, k, buf):
        gather_start(links, ("zg", s, k), ring_z, z_view(buf, k))
        to_core(s, k, buf, 0)

    def z_gather_forward(s, k, buf):
        gather_forward(links, ("zg", s, k), ring_z, z_view(buf, k))

    def z_gather_finish(s, k, buf):
        two = buf.at[k, core, 0]
        links.recv(("zg", s, k, "own"), two)
        to_core(s, k, buf, -1)
        to_core(s, k, buf, 1)
        links.recv(("zg", s, k, "far"), two)
        to_core(s, k, buf, 2)
        links.recv(("zc", s, k), buf.at[k, 1 - core])

    def encode(k):
        b0 = bk0[k].reshape(256, F0)
        b1 = bk1[k].reshape(256, features - F0)

        def tile(n, carry):
            at = pl.ds(pl.multiple_of(n * 256, 256), 256)
            out = jnp.dot(b0, enc[:F0, at], preferred_element_type=F32)
            out += jnp.dot(b1, enc[F0:, at], preferred_element_type=F32)
            parts[0, k, :, :, :, :, at] = out.astype(BF).reshape(2, 4, 2, ROWS, 256)
            return carry

        lax.fori_loop(0, 4, tile, 0)
        product_send(0, k)

    def latents(k):
        halves = z_scatter_finish(0, k)
        for h in (0, 1):
            pre = halves[h] + bias_ref[...][None, :]
            soft = jnp.maximum(pre, 0.0) + jnp.log1p(jnp.exp(-jnp.abs(pre)))
            lat[k, core, z, h] = soft.astype(BF)
            slope[k, h] = jax.nn.sigmoid(pre)
        z_gather_start(0, k, lat)

    def decode(k):
        rows = lat[k].reshape(256, -1)
        over = (((1,), (1,)), ((), ()))
        out = lax.dot_general(rows, dec[:F0], over, preferred_element_type=F32)
        rp0[k] = out.astype(BF).reshape(4, 4, ROWS, F0)
        direct_start(links, ("xs", k), ring_x, lambda q: rp0.at[k, q], lambda q: got0.at[k, q])
        out = lax.dot_general(rows, dec[F0:], over, preferred_element_type=F32)
        rp1[k] = out.astype(BF).reshape(4, 4, ROWS, features - F0)
        direct_start(links, ("ys", k), ring_y, lambda q: rp1.at[k, :, q], lambda q: got1.at[k, q])

    def recon_second(k):
        links.recv(("xs", k), got0.at[k, pl.ds(0, 3)])
        total = rp0[k, x].astype(F32)
        for shift in (1, 2, 3):
            total += got0[k, ring_x.at(shift)].astype(F32)
        s0[k] = total.astype(BF)
        direct_start(links, ("xt", k), ring_y, lambda q: s0.at[k, q], lambda q: d0.at[k, q])
        links.recv(("ys", k), got1.at[k, pl.ds(0, 3)])
        total = rp1[k, :, y].astype(F32)
        for shift in (1, 2, 3):
            total += got1[k, ring_y.at(shift)].astype(F32)
        s1[k] = total.astype(BF)
        direct_start(links, ("yt", k), ring_x, lambda q: s1.at[k, q], lambda q: d1.at[k, q])

    def recon_third(k):
        for tag, ring, s, d, q, e in (("xt", ring_y, s0, d0, q0, e0), ("yt", ring_x, s1, d1, q1, e1)):
            links.recv((tag, k), d.at[k, pl.ds(0, 3)])
            total = s[k, ring.at(0)].astype(F32)
            for shift in (1, 2, 3):
                total += d[k, ring.at(shift)].astype(F32)
            q[k] = total.astype(BF)
            links.send((tag + "z", k), q.at[k], e.at[k], zl_peer)

    def residual(k):
        own_counts = counts(bank_rows(k, x * 4 + y, ROWS))
        for tag, at, q, e, bk, rs in (
            ("xt", pl.ds(0, F0), q0, e0, bk0, rs0),
            ("yt", pl.ds(F0, features - F0), q1, e1, bk1, rs1),
        ):
            links.recv((tag + "z", k), e.at[k])
            recon = q[k].astype(F32) + e[k].astype(F32) + dbias_ref[at][None, :]
            value = (recon - bk[k, x, y].astype(F32)) * scale
            rs[k, x, y] = (value * own_counts).astype(BF)
        plane_first_start("r", k, rs0, rs1)

    def backward(k):
        r0 = rs0[k].reshape(256, F0)
        r1 = rs1[k].reshape(256, features - F0)

        def tile(n, carry):
            at = pl.ds(pl.multiple_of(n * 256, 256), 256)
            out = jnp.dot(r0, dec[:F0, at], preferred_element_type=F32)
            out += jnp.dot(r1, dec[F0:, at], preferred_element_type=F32)
            parts[1, k, :, :, :, :, at] = out.astype(BF).reshape(2, 4, 2, ROWS, 256)
            return carry

        lax.fori_loop(0, 4, tile, 0)
        product_send(1, k)

    def latent_gradient(k):
        row_counts = counts(bank_rows(k, core * 8 + z * 2, 2 * ROWS))
        total_norm = norms_ref[0:1] + norms_ref[1:2] + norms_ref[2:3]
        halves = z_scatter_finish(1, k)
        for h in (0, 1):
            weight = row_counts[h * ROWS : (h + 1) * ROWS]
            grad = halves[h] + weight * (PENALTY * scale * total_norm)
            pg[k, core, z, h] = (grad * slope[k, h]).astype(BF)
        z_gather_start(1, k, pg)

    def bank_send():
        blk0[zl] = bank_ref[:, :F0]
        blk1[zl] = bank_ref[:, F0:]
        links.send(("bz0",), blk0.at[zl], blk0.at[zl], zl_peer)
        links.send(("bz1",), blk1.at[zl], blk1.at[zl], zl_peer)

    def bank_recv():
        links.recv(("bz0",), blk0.at[1 - zl])
        links.recv(("bz1",), blk1.at[1 - zl])
        for k in range(CHUNKS):
            bk0[k, x, y] = blk0[k]
            bk1[k, x, y] = blk1[k]
            plane_first_start("b", k, bk0, bk1)

    def squares_send():
        dec_copy.wait()
        row = lax.broadcasted_iota(jnp.int32, (8, features), 0)
        column = lax.broadcasted_iota(jnp.int32, (8, features), 1) + layer * features
        owner = jnp.where((column >= row * D) & (column < (row + 1) * D), 1.0, 0.0).astype(BF)

        def square(n, carry):
            at = pl.ds(pl.multiple_of(n * 256, 256), 256)
            wide = dec[:, at].astype(F32)
            wide = wide * wide
            high = wide.astype(BF)
            low = (wide - high.astype(F32)).astype(BF)
            total = jnp.dot(owner, high, preferred_element_type=F32)
            total += jnp.dot(owner, low, preferred_element_type=F32)
            sq_part[:, at] = total
            return carry

        lax.fori_loop(0, 4, square, 0)
        links.send(("sqc",), sq_part, sq_core, core_peer)

    def squares_second():
        links.recv(("sqc",), sq_core)
        sq_chip[...] = sq_part[...] + sq_core[...]
        direct_start(links, ("sqz",), ring_z, lambda q: sq_chip, lambda q: sq_z.at[q])

    def squares_sum():
        links.recv(("sqz",), sq_z.at[pl.ds(0, 3)])
        squares = sq_chip[...]
        for shift in (1, 2, 3):
            squares += sq_z[ring_z.at(shift)]
        norms_ref[...] = jnp.sqrt(squares + 1e-6)

    def copy_out(i, src, dst):
        copy = pltpu.make_async_copy(src, dst, local_sems.at[i])
        copy.start()
        outgoing.append(copy)

    def coefficients():
        colsum = jnp.zeros((1, lat.shape[-1]), F32)
        for k in range(CHUNKS):
            weight = counts(bank_rows(k, 0, 256))
            colsum += jnp.sum(lat[k].reshape(256, -1).astype(F32) * weight, axis=0, keepdims=True)
        coef_ref[...] = (PENALTY * scale * colsum) / norms_ref[...]

    outgoing = []
    bank, resid = (bk0, bk1), (rs0, rs1)
    steps = [
        (bank_send,),
        (bank_recv,),
        (squares_send,),
        (plane_second_start, "b", 0, *bank),
        (squares_second,),
        (plane_second_start, "b", 1, *bank),
        (enc_copy.wait,),
        (plane_finish, "b", 0, *bank),
        (encode, 0),
        (z_scatter_start, 0, 0),
        (plane_finish, "b", 1, *bank),
        (encode, 1),
        (z_scatter_middle, 0, 0),
        (z_scatter_start, 0, 1),
        (copy_out, 2, bk0, bank0_out),
        (copy_out, 3, bk1, bank1_out),
        (squares_sum,),
        (latents, 0),
        (z_scatter_middle, 0, 1),
        (z_gather_forward, 0, 0, lat),
        (latents, 1),
        (z_gather_finish, 0, 0, lat),
        (decode, 0),
        (z_gather_forward, 0, 1, lat),
        (z_gather_finish, 0, 1, lat),
        (decode, 1),
        (recon_second, 0),
        (recon_third, 0),
        (recon_second, 1),
        (residual, 0),
        (recon_third, 1),
        (plane_second_start, "r", 0, *resid),
        (residual, 1),
        (copy_out, 4, lat, lat_out),
        (plane_second_start, "r", 1, *resid),
        (plane_finish, "r", 0, *resid),
        (backward, 0),
        (z_scatter_start, 1, 0),
        (plane_finish, "r", 1, *resid),
        (backward, 1),
        (z_scatter_middle, 1, 0),
        (z_scatter_start, 1, 1),
        (copy_out, 5, rs0, res0_out),
        (copy_out, 6, rs1, res1_out),
        (latent_gradient, 0),
        (z_scatter_middle, 1, 1),
        (z_gather_forward, 1, 0, pg),
        (latent_gradient, 1),
        (coefficients,),
        (z_gather_finish, 1, 0, pg),
        (z_gather_forward, 1, 1, pg),
        (z_gather_finish, 1, 1, pg),
        (copy_out, 7, pg, pg_out),
    ]
    for step, *given in steps:
        step(*given)
    for family, view in (
        ("bz0", blk0.at[0]),
        ("bz1", blk1.at[0]),
        ("b0", s0.at[:, pl.ds(0, 3)]),
        ("b1", s1.at[:, pl.ds(0, 3)]),
        ("b2", got0.at[:, pl.ds(0, 3)]),
        ("b3", got1.at[:, pl.ds(0, 3)]),
        ("sqc", sq_part),
        ("sqz", sq_z.at[pl.ds(0, 3)]),
        ("core", sums),
        ("zs", zgot),
        ("zg", zgot),
        ("zc", sums),
        ("xs", got0.at[:, pl.ds(0, 3)]),
        ("ys", got1.at[:, pl.ds(0, 3)]),
        ("xt", s0.at[:, pl.ds(0, 3)]),
        ("yt", s1.at[:, pl.ds(0, 3)]),
        ("xtz", q0),
        ("ytz", q1),
        ("r0", s0.at[:, pl.ds(0, 3)]),
        ("r1", s1.at[:, pl.ds(0, 3)]),
        ("r2", got0.at[:, pl.ds(0, 3)]),
        ("r3", got1.at[:, pl.ds(0, 3)]),
    ):
        links.sent(family, view)
    for copy in outgoing:
        copy.wait()


def shards(ids, bank, enc_weight, enc_bias, dec_weight, dec_bias):
    tokens = ids.shape[0]
    features, lats = enc_weight.shape
    dec = dec_weight.T
    f1 = features - F0
    scale = 1.0 / math.sqrt(tokens)
    k = CHUNKS
    vmem = pl.BlockSpec(memory_space=pltpu.VMEM)
    hbm = pl.BlockSpec(memory_space=pl.ANY)
    messages = 68
    bank0, bank1, lat, res0, res1, pg, coef = pl.pallas_call(
        functools.partial(kernel, scale),
        out_shape=[
            jax.ShapeDtypeStruct((k, 4, 4, ROWS, F0), BF),
            jax.ShapeDtypeStruct((k, 4, 4, ROWS, f1), BF),
            jax.ShapeDtypeStruct((k, 2, 4, 2, ROWS, lats), BF),
            jax.ShapeDtypeStruct((k, 4, 4, ROWS, F0), BF),
            jax.ShapeDtypeStruct((k, 4, 4, ROWS, f1), BF),
            jax.ShapeDtypeStruct((k, 2, 4, 2, ROWS, lats), BF),
            jax.ShapeDtypeStruct((8, lats), F32),
        ],
        in_specs=[vmem, vmem, vmem, vmem, hbm, hbm],
        out_specs=[hbm] * 6 + [vmem],
        scratch_shapes=[
            pltpu.VMEM((features, lats), BF),
            pltpu.VMEM((features, lats), BF),
            pltpu.VMEM((2, ROWS, F0), BF),
            pltpu.VMEM((2, ROWS, f1), BF),
            pltpu.VMEM((k, 4, 4, ROWS, F0), BF),
            pltpu.VMEM((k, 4, 4, ROWS, f1), BF),
            pltpu.VMEM((2, k, 2, 4, 2, ROWS, lats), BF),
            pltpu.VMEM((2, k, 4, 2, ROWS, lats), BF),
            pltpu.VMEM((2, k, 4, 2, ROWS, lats), BF),
            pltpu.VMEM((2, k, 6, ROWS, lats), BF),
            pltpu.VMEM((2, k, 2, ROWS, lats), BF),
            pltpu.VMEM((k, 2, 4, 2, ROWS, lats), BF),
            pltpu.VMEM((k, 2, 4, 2, ROWS, lats), BF),
            pltpu.VMEM((k, 2, ROWS, lats), F32),
            pltpu.VMEM((k, 4, 4, ROWS, F0), BF),
            pltpu.VMEM((k, 4, 4, ROWS, f1), BF),
            pltpu.VMEM((k, 4, 4, ROWS, F0), BF),
            pltpu.VMEM((k, 4, 4, ROWS, f1), BF),
            pltpu.VMEM((k, 4, ROWS, F0), BF),
            pltpu.VMEM((k, 4, ROWS, f1), BF),
            pltpu.VMEM((k, 4, ROWS, F0), BF),
            pltpu.VMEM((k, 4, ROWS, f1), BF),
            pltpu.VMEM((k, ROWS, F0), BF),
            pltpu.VMEM((k, ROWS, f1), BF),
            pltpu.VMEM((k, ROWS, F0), BF),
            pltpu.VMEM((k, ROWS, f1), BF),
            pltpu.VMEM((k, 4, 4, ROWS, F0), BF),
            pltpu.VMEM((k, 4, 4, ROWS, f1), BF),
            pltpu.VMEM((8, lats), F32),
            pltpu.VMEM((8, lats), F32),
            pltpu.VMEM((8, lats), F32),
            pltpu.VMEM((4, 8, lats), F32),
            pltpu.VMEM((8, lats), F32),
            pltpu.SemaphoreType.DMA((22,)),
            pltpu.SemaphoreType.DMA((messages,)),
            pltpu.SemaphoreType.DMA((8,)),
        ],
        compiler_params=pltpu.CompilerParams(
            collective_id=0, has_side_effects=True, vmem_limit_bytes=56 * 2**20
        ),
        name="crosscoder_step",
    )(ids, bank, enc_bias, dec_bias, enc_weight, dec)

    grad_encoder, grad_decoder = gradients(bank0, bank1, res0, res1, lat, pg, coef, dec)
    return grad_encoder, grad_decoder.T


def gradients_kernel(bank0, bank1, res0, res1, lat, pg, coef, dec, enc_grad, dec_grad):
    features = enc_grad.shape[0]
    over = (((0,), (0,)), ((), ()))
    rows = lat.shape[0]
    start = lax.axis_index("layer") * features
    for at, bank, res in ((0, bank0, res0), (F0, bank1, res1)):
        size = bank.shape[-1]
        span = pl.ds(at, size)
        right = lat[...]
        out = lax.dot_general(res[...], right, over, preferred_element_type=F32)
        feature = start + at + lax.broadcasted_iota(jnp.int32, (size, 1), 0)
        spread = jnp.where(
            feature < D, coef[0:1], jnp.where(feature < 2 * D, coef[1:2], coef[2:3])
        )
        dec_grad[span] = (out + spread * dec[span].astype(F32)).astype(BF)
        out = lax.dot_general(bank[...], pg[...], over, preferred_element_type=F32)
        enc_grad[span] = out.astype(BF)


def gradients(bank0, bank1, res0, res1, lat, pg, coef, dec):
    features, lats = dec.shape
    tile = 256
    whole = lambda a: pl.BlockSpec((a.shape[0], a.shape[1]), lambda n: (0, 0))
    piece = lambda a: pl.BlockSpec((a.shape[0], tile), lambda n: (0, n))
    bank0, bank1, res0, res1 = (a.reshape(-1, a.shape[-1]) for a in (bank0, bank1, res0, res1))
    lat, pg = lat.reshape(-1, lats), pg.reshape(-1, lats)
    out = jax.ShapeDtypeStruct((features, lats), BF)
    return pl.pallas_call(
        gradients_kernel,
        out_shape=[out, out],
        grid=(lats // tile,),
        in_specs=[whole(a) for a in (bank0, bank1, res0, res1)]
        + [piece(a) for a in (lat, pg, coef, dec)],
        out_specs=[piece(out), piece(out)],
        compiler_params=pltpu.CompilerParams(vmem_limit_bytes=56 * 2**20),
        name="gradients",
    )(bank0, bank1, res0, res1, lat, pg, coef, dec)


def solution(mesh):
    in_specs = (
        P(),
        P("latent", "layer"),
        P("layer", "latent"),
        P("latent"),
        P("latent", "layer"),
        P("layer"),
    )
    out_specs = (P("layer", "latent"), P("latent", "layer"))
    return jax.shard_map(shards, mesh=mesh, in_specs=in_specs, out_specs=out_specs, check_vma=False)
```

time: 129 us -> 114 us (0.88)
  matrix products: 8.72 us -> 0 us
  local copies, waits for them, and re-layouts: 6.71 us -> 0 us
    dot_general x2 -> x0, matrix products: 8.72 us -> none  [the longest x1 5.54 us: shards(): lax.dot_general(lat.reshape(-1, lats), resid, over, preferred_element_typ...]
    pallas_call x0 -> x1, Pallas kernels: none -> 8.08 us  [gradients(): pl.pallas_call(gradients_kernel, out_shape=[out, out], grid=(lats // tile...]
    pallas_call x1, Pallas kernels: 112 us -> 104 us  [shards(): pl.pallas_call(functools.partial(kernel, scale), out_shape=[jax.ShapeDtyp...]
    unnamed x9 -> x0, local copies, waits for them, and re-layouts: 4.54 us -> none
    broadcast_in_dim x1 -> x0, local copies, waits for them, and re-layouts: 1.3 us -> none  [shards(): dec_bias[None, :]]
where the time goes in v2:
time: 114 us; the launch traced here: 113 us
  Pallas kernels  112 us (98%)
    pallas_call x1, Pallas kernels, shards(): pl.pallas_call(functools.partial(kernel, scale), out_shape=[jax.ShapeDtyp...  104 us
    pallas_call x1, Pallas kernels, gradients(): pl.pallas_call(gradients_kernel, out_shape=[out, out], grid=(lats // tile...  8.08 us

profile of v2, /device:TPU:1, one launch (start us, length us, event | category | flops | bytes accessed | tf_op | source)
XLA Modules:
  0.0 113.0 jit_solution(6411657741087277403)
XLA Ops:
  0.6 104.3 %crosscoder_step.1 = (bf16[2,4,4,16,640]{4,3,2,1,0:T(8,128)(2,1)}, bf16[2,4,4,16,704]{4,3,2,1,0:T(8,128)(2,1)}, bf16[2,2,4,2,16,1024]{5,4,3,2,1,0:T(8,128)(2,1)}...) custom-call(s32[512]{0:T(512)} %ids_ref.1, ...), custom_call_target="tpu_custom_call" | custom-call | tf_op jit(solution)/shard_map/crosscoder_step/pallas_call | solution.py:464
  104.9 8.1 %gradients.1 = (bf16[1344,1024]{1,0:T(8,128)(2,1)}, bf16[1344,1024]{1,0:T(8,128)(2,1)}) custom-call(bf16[512,640]{1,0:T(8,128)(2,1)} %bitcast.14, bf16[512,704]{1,0:T(8,128)(2,1)} %bitcast.12, bf16[512,640]{1,0:T(8,128)(2,1)} %bitcast.15, bf16[512,704]{1,0:T(8,128)(2,1)} %bitcast.13, bf16[512,1024]{1,0:T(8,128)(2,1)} %bitcast.10, ...), custom_call_target="tpu_custom_call" | custom-call | tf_op jit(solution)/shard_map/gradients/pallas_call | solution.py:552

commit v3 on v2

--- a/solution.py
+++ b/solution.py
@@ -14,6 +14,8 @@
 ROWS = 16
 F0 = 640
 CHUNKS = 2
+Z_RS = "ring"
+Z_AG = "ring"
 MESH = pl.DeviceIdType.MESH
 BF = jnp.bfloat16
 F32 = jnp.float32
@@ -105,12 +107,12 @@
 
 def kernel(
     scale,
-    ids_ref, bank_ref, bias_ref, dbias_ref, enc_hbm, dec_hbm,
-    bank0_out, bank1_out, lat_out, res0_out, res1_out, pg_out, coef_ref,
-    enc, dec, blk0, blk1, bk0, bk1,
+    ids_hbm, bank_hbm, bias_hbm, dbias_hbm, enc_hbm, dec_hbm,
+    turned_out, dgrad_out, pg_out,
+    ids_ref, bank_ref, bias_ref, dbias_ref, enc, dec, blk0, blk1, bk0, bk1,
     parts, from_core, sums, zgot, zboth, lat, pg, slope,
     rp0, rp1, got0, got1, s0, s1, d0, d1, q0, q1, e0, e1, rs0, rs1,
-    sq_part, sq_core, sq_chip, sq_z, norms_ref,
+    sq_part, sq_core, sq_chip, sq_z, norms_ref, coef_ref, turned, resid_turned, dgrad,
     send_sems, recv_sems, local_sems,
 ):
     layer, latent = lax.axis_index("layer"), lax.axis_index("latent")
@@ -127,8 +129,13 @@
 
     dec_copy = pltpu.make_async_copy(dec_hbm, dec, local_sems.at[0])
     enc_copy = pltpu.make_async_copy(enc_hbm, enc, local_sems.at[1])
-    dec_copy.start()
-    enc_copy.start()
+    bank_copy = pltpu.make_async_copy(bank_hbm, bank_ref, local_sems.at[5])
+    small_copies = [
+        pltpu.make_async_copy(src, dst, local_sems.at[6 + i])
+        for i, (src, dst) in enumerate(((ids_hbm, ids_ref), (bias_hbm, bias_ref), (dbias_hbm, dbias_ref)))
+    ]
+    for copy in (bank_copy, *small_copies, dec_copy, enc_copy):
+        copy.start()
 
     partners = [core_peer, zl_peer]
     for ring in (ring_x, ring_y, ring_z):
@@ -184,32 +191,58 @@
         links.recv(("core", s, k), from_core.at[s, k])
         own = parts[s, k, core].astype(F32) + from_core[s, k].astype(F32)
         sums[s, k] = own.astype(BF)
-        scatter_start(links, ("zs", s, k), ring_z, z_part(s, k), z_got(s, k))
+        if Z_RS == "ring":
+            scatter_start(links, ("zs", s, k), ring_z, z_part(s, k), z_got(s, k))
+        else:
+            direct_start(
+                links,
+                ("zs", s, k),
+                ring_z,
+                lambda q: sums.at[s, k, q],
+                lambda q: zgot.at[s, k, pl.ds(2 * q, 2)],
+            )
 
     def z_scatter_middle(s, k):
-        scatter_middle(links, ("zs", s, k), ring_z, z_part(s, k), z_got(s, k), z_both(s, k))
+        if Z_RS == "ring":
+            scatter_middle(links, ("zs", s, k), ring_z, z_part(s, k), z_got(s, k), z_both(s, k))
 
     def z_scatter_finish(s, k):
-        last_four = zgot.at[s, k, pl.ds(2, 4)]
-        return scatter_finish(links, ("zs", s, k), ring_z, z_part(s, k), z_got(s, k), last_four)
+        if Z_RS == "ring":
+            last_four = zgot.at[s, k, pl.ds(2, 4)]
+            return scatter_finish(links, ("zs", s, k), ring_z, z_part(s, k), z_got(s, k), last_four)
+        links.recv(("zs", s, k), zgot.at[s, k, pl.ds(0, 6)])
+        total = sums[s, k, z].astype(F32)
+        for shift in (1, 2, 3):
+            total += zgot[s, k, pl.ds(2 * ring_z.at(shift), 2)].astype(F32)
+        return total[0], total[1]
 
     def to_core(s, k, buf, shift):
         block = buf.at[k, core, ring_z.at(shift)]
         links.send(("zc", s, k), block, block, core_peer)
 
     def z_gather_start(s, k, buf):
-        gather_start(links, ("zg", s, k), ring_z, z_view(buf, k))
+        if Z_AG == "ring":
+            gather_start(links, ("zg", s, k), ring_z, z_view(buf, k))
+        else:
+            own = buf.at[k, core, z]
+            direct_start(links, ("zg", s, k), ring_z, lambda q: own, lambda q: buf.at[k, core, q])
         to_core(s, k, buf, 0)
 
     def z_gather_forward(s, k, buf):
-        gather_forward(links, ("zg", s, k), ring_z, z_view(buf, k))
+        if Z_AG == "ring":
+            gather_forward(links, ("zg", s, k), ring_z, z_view(buf, k))
 
     def z_gather_finish(s, k, buf):
         two = buf.at[k, core, 0]
-        links.recv(("zg", s, k, "own"), two)
-        to_core(s, k, buf, -1)
-        to_core(s, k, buf, 1)
-        links.recv(("zg", s, k, "far"), two)
+        if Z_AG == "ring":
+            links.recv(("zg", s, k, "own"), two)
+            to_core(s, k, buf, -1)
+            to_core(s, k, buf, 1)
+            links.recv(("zg", s, k, "far"), two)
+        else:
+            links.recv(("zg", s, k), buf.at[k, core, pl.ds(0, 3)])
+            to_core(s, k, buf, -1)
+            to_core(s, k, buf, 1)
         to_core(s, k, buf, 2)
         links.recv(("zc", s, k), buf.at[k, 1 - core])
 
@@ -306,6 +339,7 @@
         z_gather_start(1, k, pg)
 
     def bank_send():
+        bank_copy.wait()
         blk0[zl] = bank_ref[:, :F0]
         blk1[zl] = bank_ref[:, F0:]
         links.send(("bz0",), blk0.at[zl], blk0.at[zl], zl_peer)
@@ -320,7 +354,8 @@
             plane_first_start("b", k, bk0, bk1)
 
     def squares_send():
-        dec_copy.wait()
+        for copy in (*small_copies, dec_copy):
+            copy.wait()
         row = lax.broadcasted_iota(jnp.int32, (8, features), 0)
         column = lax.broadcasted_iota(jnp.int32, (8, features), 1) + layer * features
         owner = jnp.where((column >= row * D) & (column < (row + 1) * D), 1.0, 0.0).astype(BF)
@@ -362,6 +397,28 @@
             weight = counts(bank_rows(k, 0, 256))
             colsum += jnp.sum(lat[k].reshape(256, -1).astype(F32) * weight, axis=0, keepdims=True)
         coef_ref[...] = (PENALTY * scale * colsum) / norms_ref[...]
+
+    def turn(buf, k, pair):
+        at = pl.ds(256 * k, 256)
+        buf[:F0, at] = pair[0][k].reshape(256, F0).T
+        buf[F0:, at] = pair[1][k].reshape(256, features - F0).T
+
+    def decoder_gradient(first, last):
+        feature = layer * features + lax.broadcasted_iota(jnp.int32, (features, 1), 0)
+
+        def tile(n, carry):
+            at = pl.ds(pl.multiple_of(n * 256, 256), 256)
+            out = jnp.zeros((features, 256), F32)
+            for k in range(CHUNKS):
+                rows = lat[k, :, :, :, :, at].reshape(256, 256)
+                out += jnp.dot(resid_turned[:, 256 * k : 256 * k + 256], rows, preferred_element_type=F32)
+            spread = jnp.where(
+                feature < D, coef_ref[0:1, at], jnp.where(feature < 2 * D, coef_ref[1:2, at], coef_ref[2:3, at])
+            )
+            dgrad[:, at] = (out + spread * dec[:, at].astype(F32)).astype(BF)
+            return carry
+
+        lax.fori_loop(first, last, tile, 0)
 
     outgoing = []
     bank, resid = (bk0, bk1), (rs0, rs1)
@@ -380,8 +437,9 @@
         (encode, 1),
         (z_scatter_middle, 0, 0),
         (z_scatter_start, 0, 1),
-        (copy_out, 2, bk0, bank0_out),
-        (copy_out, 3, bk1, bank1_out),
+        (turn, turned, 0, bank),
+        (turn, turned, 1, bank),
+        (copy_out, 2, turned, turned_out),
         (squares_sum,),
         (latents, 0),
         (z_scatter_middle, 0, 1),
@@ -392,6 +450,7 @@
         (z_gather_forward, 0, 1, lat),
         (z_gather_finish, 0, 1, lat),
         (decode, 1),
+        (coefficients,),
         (recon_second, 0),
         (recon_third, 0),
         (recon_second, 1),
@@ -399,26 +458,27 @@
         (recon_third, 1),
         (plane_second_start, "r", 0, *resid),
         (residual, 1),
-        (copy_out, 4, lat, lat_out),
         (plane_second_start, "r", 1, *resid),
         (plane_finish, "r", 0, *resid),
         (backward, 0),
         (z_scatter_start, 1, 0),
+        (turn, resid_turned, 0, resid),
         (plane_finish, "r", 1, *resid),
         (backward, 1),
         (z_scatter_middle, 1, 0),
         (z_scatter_start, 1, 1),
-        (copy_out, 5, rs0, res0_out),
-        (copy_out, 6, rs1, res1_out),
+        (turn, resid_turned, 1, resid),
+        (decoder_gradient, 0, 2),
         (latent_gradient, 0),
         (z_scatter_middle, 1, 1),
         (z_gather_forward, 1, 0, pg),
         (latent_gradient, 1),
-        (coefficients,),
+        (decoder_gradient, 2, 4),
+        (copy_out, 3, dgrad, dgrad_out),
         (z_gather_finish, 1, 0, pg),
         (z_gather_forward, 1, 1, pg),
         (z_gather_finish, 1, 1, pg),
-        (copy_out, 7, pg, pg_out),
+        (copy_out, 4, pg, pg_out),
     ]
     for step, *given in steps:
         step(*given)
@@ -432,8 +492,8 @@
         ("sqc", sq_part),
         ("sqz", sq_z.at[pl.ds(0, 3)]),
         ("core", sums),
-        ("zs", zgot),
-        ("zg", zgot),
+        ("zs", zgot.at[:, :, pl.ds(0, 6)]),
+        ("zg", zgot.at[:, :, pl.ds(0, 6)]),
         ("zc", sums),
         ("xs", got0.at[:, pl.ds(0, 3)]),
         ("ys", got1.at[:, pl.ds(0, 3)]),
@@ -458,23 +518,22 @@
     f1 = features - F0
     scale = 1.0 / math.sqrt(tokens)
     k = CHUNKS
-    vmem = pl.BlockSpec(memory_space=pltpu.VMEM)
-    hbm = pl.BlockSpec(memory_space=pl.ANY)
+    operands = (ids, bank, enc_bias, dec_bias, enc_weight, dec)
     messages = 68
-    bank0, bank1, lat, res0, res1, pg, coef = pl.pallas_call(
+    turned, dgrad, pg = pl.pallas_call(
         functools.partial(kernel, scale),
         out_shape=[
-            jax.ShapeDtypeStruct((k, 4, 4, ROWS, F0), BF),
-            jax.ShapeDtypeStruct((k, 4, 4, ROWS, f1), BF),
+            jax.ShapeDtypeStruct((features, k * 256), BF),
+            jax.ShapeDtypeStruct((features, lats), BF),
             jax.ShapeDtypeStruct((k, 2, 4, 2, ROWS, lats), BF),
-            jax.ShapeDtypeStruct((k, 4, 4, ROWS, F0), BF),
-            jax.ShapeDtypeStruct((k, 4, 4, ROWS, f1), BF),
-            jax.ShapeDtypeStruct((k, 2, 4, 2, ROWS, lats), BF),
-            jax.ShapeDtypeStruct((8, lats), F32),
         ],
-        in_specs=[vmem, vmem, vmem, vmem, hbm, hbm],
-        out_specs=[hbm] * 6 + [vmem],
+        in_specs=[pl.BlockSpec(memory_space=pl.ANY)] * 6,
+        out_specs=[pl.BlockSpec(memory_space=pl.ANY)] * 3,
         scratch_shapes=[
+            pltpu.VMEM(ids.shape, jnp.int32),
+            pltpu.VMEM(bank.shape, BF),
+            pltpu.VMEM(enc_bias.shape, F32),
+            pltpu.VMEM(dec_bias.shape, F32),
             pltpu.VMEM((features, lats), BF),
             pltpu.VMEM((features, lats), BF),
             pltpu.VMEM((2, ROWS, F0), BF),
@@ -484,7 +543,7 @@
             pltpu.VMEM((2, k, 2, 4, 2, ROWS, lats), BF),
             pltpu.VMEM((2, k, 4, 2, ROWS, lats), BF),
             pltpu.VMEM((2, k, 4, 2, ROWS, lats), BF),
-            pltpu.VMEM((2, k, 6, ROWS, lats), BF),
+            pltpu.VMEM((2, k, 8, ROWS, lats), BF),
             pltpu.VMEM((2, k, 2, ROWS, lats), BF),
             pltpu.VMEM((k, 2, 4, 2, ROWS, lats), BF),
             pltpu.VMEM((k, 2, 4, 2, ROWS, lats), BF),
@@ -508,57 +567,43 @@
             pltpu.VMEM((8, lats), F32),
             pltpu.VMEM((4, 8, lats), F32),
             pltpu.VMEM((8, lats), F32),
+            pltpu.VMEM((8, lats), F32),
+            pltpu.VMEM((features, k * 256), BF),
+            pltpu.VMEM((features, k * 256), BF),
+            pltpu.VMEM((features, lats), BF),
             pltpu.SemaphoreType.DMA((22,)),
             pltpu.SemaphoreType.DMA((messages,)),
-            pltpu.SemaphoreType.DMA((8,)),
+            pltpu.SemaphoreType.DMA((9,)),
         ],
         compiler_params=pltpu.CompilerParams(
-            collective_id=0, has_side_effects=True, vmem_limit_bytes=56 * 2**20
+            collective_id=0, has_side_effects=True, vmem_limit_bytes=40 * 2**20
         ),
         name="crosscoder_step",
-    )(ids, bank, enc_bias, dec_bias, enc_weight, dec)
-
-    grad_encoder, grad_decoder = gradients(bank0, bank1, res0, res1, lat, pg, coef, dec)
+    )(*(pltpu.with_memory_space_constraint(a, pltpu.HBM) for a in operands))
+
+    grad_encoder, grad_decoder = gradients(turned, pg.reshape(-1, lats), dgrad)
     return grad_encoder, grad_decoder.T
 
 
-def gradients_kernel(bank0, bank1, res0, res1, lat, pg, coef, dec, enc_grad, dec_grad):
-    features = enc_grad.shape[0]
-    over = (((0,), (0,)), ((), ()))
-    rows = lat.shape[0]
-    start = lax.axis_index("layer") * features
-    for at, bank, res in ((0, bank0, res0), (F0, bank1, res1)):
-        size = bank.shape[-1]
-        span = pl.ds(at, size)
-        right = lat[...]
-        out = lax.dot_general(res[...], right, over, preferred_element_type=F32)
-        feature = start + at + lax.broadcasted_iota(jnp.int32, (size, 1), 0)
-        spread = jnp.where(
-            feature < D, coef[0:1], jnp.where(feature < 2 * D, coef[1:2], coef[2:3])
-        )
-        dec_grad[span] = (out + spread * dec[span].astype(F32)).astype(BF)
-        out = lax.dot_general(bank[...], pg[...], over, preferred_element_type=F32)
-        enc_grad[span] = out.astype(BF)
-
-
-def gradients(bank0, bank1, res0, res1, lat, pg, coef, dec):
-    features, lats = dec.shape
-    tile = 256
-    whole = lambda a: pl.BlockSpec((a.shape[0], a.shape[1]), lambda n: (0, 0))
-    piece = lambda a: pl.BlockSpec((a.shape[0], tile), lambda n: (0, n))
-    bank0, bank1, res0, res1 = (a.reshape(-1, a.shape[-1]) for a in (bank0, bank1, res0, res1))
-    lat, pg = lat.reshape(-1, lats), pg.reshape(-1, lats)
-    out = jax.ShapeDtypeStruct((features, lats), BF)
+def gradients_kernel(turned, pg, dgrad, enc_grad, dec_grad):
+    dec_grad[...] = dgrad[...]
+    enc_grad[...] = jnp.dot(turned[...], pg[...], preferred_element_type=F32).astype(BF)
+
+
+def gradients(turned, pg, dgrad):
+    features, lats = dgrad.shape
+    size = features // 3
+    piece = lambda a: pl.BlockSpec((size, a.shape[1]), lambda n: (n, 0))
+    whole = pl.BlockSpec(pg.shape, lambda n: (0, 0))
     return pl.pallas_call(
         gradients_kernel,
-        out_shape=[out, out],
-        grid=(lats // tile,),
-        in_specs=[whole(a) for a in (bank0, bank1, res0, res1)]
-        + [piece(a) for a in (lat, pg, coef, dec)],
-        out_specs=[piece(out), piece(out)],
-        compiler_params=pltpu.CompilerParams(vmem_limit_bytes=56 * 2**20),
+        out_shape=[jax.ShapeDtypeStruct(dgrad.shape, BF)] * 2,
+        grid=(3,),
+        in_specs=[piece(turned), whole, piece(dgrad)],
+        out_specs=[piece(dgrad), piece(dgrad)],
+        compiler_params=pltpu.CompilerParams(vmem_limit_bytes=24 * 2**20),
         name="gradients",
-    )(bank0, bank1, res0, res1, lat, pg, coef, dec)
+    )(turned, pg, dgrad)
 
 
 def solution(mesh):

time: 114 us -> 109 us (0.956)
  Pallas kernels: 112 us -> 108 us
    pallas_call x1, Pallas kernels: 8.08 us -> 3.74 us  [gradients(): pl.pallas_call(gradients_kernel, out_shape=[jax.ShapeDtypeStruct(dgrad.sh...]
where the time goes in v3:
time: 109 us; the launch traced here: 108 us
  Pallas kernels  108 us (99%)
    pallas_call x1, Pallas kernels, shards(): pl.pallas_call(functools.partial(kernel, scale), out_shape=[jax.ShapeDtyp...  104 us
    pallas_call x1, Pallas kernels, gradients(): pl.pallas_call(gradients_kernel, out_shape=[jax.ShapeDtypeStruct(dgrad.sh...  3.74 us

profile of v3, /device:TPU:1, one launch (start us, length us, event | category | flops | bytes accessed | tf_op | source)
XLA Modules:
  0.0 108.4 jit_solution(14456439448367440889)
XLA Ops:
  0.6 104.0 %crosscoder_step.1 = (bf16[1344,512]{1,0:T(8,128)(2,1)S(1)}, bf16[1344,1024]{1,0:T(8,128)(2,1)S(1)}, bf16[2,2,4,2,16,1024]{5,4,3,2,1,0:T(8,128)(2,1)S(1)}) custom-call(s32[512]{0:T(512)} %ids_hbm.1, bf16[16,1344]{1,0:T(8,128)(2,1)} %bank_hbm.1, f32[1024]{0:T(1024)} %bias_hbm.1, f32[1344]{0:T(1024)} %dbias_hbm.1, bf16[1344,1024]{1,0:T(8,128)(2,1)} %enc_hbm.1, ...), custom_call_target="tpu_custom_call" | custom-call | tf_op jit(solution)/shard_map/crosscoder_step/pallas_call | solution.py:523
  104.7 3.7 %gradients.1 = (bf16[1344,1024]{1,0:T(8,128)(2,1)}, bf16[1344,1024]{1,0:T(8,128)(2,1)}) custom-call(bf16[1344,512]{1,0:T(8,128)(2,1)S(1)} %get-tuple-element.7.turned, bf16[512,1024]{1,0:T(8,128)(2,1)S(1)} %bitcast.3, bf16[1344,1024]{1,0:T(8,128)(2,1)S(1)} %get-tuple-element.9.dgrad), custom_call_target="tpu_custom_call" | custom-call | tf_op jit(solution)/shard_map/gradients/pallas_call | solution.py:598

commit v4 on v0

v4 whole, which is shorter than its diff:
```python
import functools
import math

import jax
import jax.numpy as jnp
from jax import lax
from jax.experimental import pallas as pl
from jax.experimental.pallas import tpu as pltpu
from jax.sharding import PartitionSpec as P

D = 3584
LAYERS = 3
PENALTY = 0.3
ROWS = 16
F0 = 640
CHUNKS = 4
LAG = 4.5
MESH = pl.DeviceIdType.MESH
BF = jnp.bfloat16
F32 = jnp.float32


class Links:
    def __init__(self, send_sems, recv_sems, me):
        self.send_sems, self.recv_sems, self.me = send_sems, recv_sems, me
        self.names, self.families = {}, {}

    def copy(self, name, src, dst, device):
        i = self.names.setdefault(name, len(self.names))
        j = self.families.setdefault(name[0], len(self.families))
        return pltpu.make_async_remote_copy(
            src_ref=src,
            dst_ref=dst,
            send_sem=self.send_sems.at[j],
            recv_sem=self.recv_sems.at[i],
            device_id=device,
            device_id_type=MESH,
        )

    def send(self, name, src, dst, device):
        self.copy(name, src, dst, device).start()

    def recv(self, name, view):
        self.copy(name, view, view, self.me).wait_recv()

    def sent(self, family, view):
        i = self.families[family]
        pltpu.make_async_copy(view, view, self.send_sems.at[i]).wait()


class Ring:
    def __init__(self, place, device_at):
        self.place, self.device_at = place, device_at

    def at(self, shift):
        return lax.rem(self.place + shift % 4, 4)

    def device(self, shift):
        return self.device_at(self.at(shift))


def direct_start(links, tag, ring, source, target):
    for d in (2, 1, 3):
        links.send(tag, source(ring.at(d)), target(ring.at(0)), ring.device(d))


def kernel(
    scale,
    ids_hbm, bank_hbm, bias_hbm, dbias_hbm, enc_hbm, dec_hbm,
    turned_out, dgrad_out, pg_out,
    ids_ref, bank_ref, bias_ref, dbias_ref, enc, dec, blk0, blk1, bk0, bk1,
    parts, from_core, sums, zgot, lat, pg, slope,
    rp0, rp1, got0, got1, s0, s1, d0, d1, q0, q1, e0, e1, rs0, rs1,
    sq_part, sq_core, sq_chip, sq_z, norms_ref, coef_ref, turned, resid_turned, dgrad,
    send_sems, recv_sems, local_sems,
):
    layer, latent = lax.axis_index("layer"), lax.axis_index("latent")
    z, core = layer // 2, lax.rem(layer, 2)
    x, y = latent // 8, lax.rem(latent, 4)
    zl = lax.rem(latent // 4, 2)
    features = enc.shape[0]
    ring_z = Ring(z, lambda q: (q * 2 + core, latent))
    ring_x = Ring(x, lambda q: (layer, q * 8 + zl * 4 + y))
    ring_y = Ring(y, lambda q: (layer, x * 8 + zl * 4 + q))
    core_peer = (z * 2 + 1 - core, latent)
    zl_peer = (layer, x * 8 + (1 - zl) * 4 + y)
    links = Links(send_sems, recv_sems, (layer, latent))

    dec_copy = pltpu.make_async_copy(dec_hbm, dec, local_sems.at[0])
    enc_copy = pltpu.make_async_copy(enc_hbm, enc, local_sems.at[1])
    bank_copy = pltpu.make_async_copy(bank_hbm, bank_ref, local_sems.at[5])
    small_copies = [
        pltpu.make_async_copy(src, dst, local_sems.at[6 + i])
        for i, (src, dst) in enumerate(((ids_hbm, ids_ref), (bias_hbm, bias_ref), (dbias_hbm, dbias_ref)))
    ]
    for copy in (bank_copy, *small_copies, dec_copy, enc_copy):
        copy.start()

    partners = [core_peer, zl_peer]
    for ring in (ring_x, ring_y, ring_z):
        partners += [ring.device(d) for d in (1, 2, 3)]
    barrier = pltpu.get_barrier_semaphore()
    for device in partners:
        pl.semaphore_signal(barrier, inc=1, device_id=device, device_id_type=MESH)
    pl.semaphore_wait(barrier, len(partners))

    def counts(rows):
        hits = (ids_ref[...][None, :] == rows).astype(F32)
        return jnp.sum(hits, axis=1, keepdims=True)

    def bank_rows(k, block, n, stride=1):
        i = lax.broadcasted_iota(jnp.int32, (n, 1), 0)
        j = block + stride * (i // ROWS)
        at_x = j // 2
        at_y = 2 * lax.rem(j, 2) + lax.rem(at_x + k % 2, 2)
        return ((at_x * 2 + k // 2) * 4 + at_y) * ROWS + lax.rem(i, ROWS)

    def first(buf, k, q):
        return buf.at[k, q]

    def other(buf, k, q):
        return buf.at[k, :, lax.rem(q + k % 2, 2), q // 2]

    def bank_first(k, q):
        return bk0.at[k // 2, q, :, lax.rem(q + k % 2, 2)]

    def bank_other(k, q):
        return bk1.at[k // 2, :, lax.rem(q + k % 2, 2), q]

    def bank_spread(k):
        direct_start(links, ("b2", k), ring_x, lambda q: bank_first(k, x), lambda q: bank_first(k, q))
        direct_start(links, ("b3", k), ring_y, lambda q: bank_other(k, y), lambda q: bank_other(k, q))

    def bank_chunk(k):
        low, odd = k // 2, k % 2
        places = [(i, 2 * j + (i + odd) % 2) for i in range(4) for j in range(2)]
        b0 = [bk0[low, i, j // 2, j % 2] for i, j in places]
        b1 = [bk1[low, i // 2, i % 2, j] for i, j in places]
        return jnp.concatenate(b0, axis=0), jnp.concatenate(b1, axis=0)

    def product(s, k, left, weight):
        def tile(n, carry):
            at = pl.ds(pl.multiple_of(n * 256, 256), 256)
            out = jnp.dot(left[0], weight[:F0, at], preferred_element_type=F32)
            out += jnp.dot(left[1], weight[F0:, at], preferred_element_type=F32)
            parts[s, k, :, :, :, at] = out.astype(BF).reshape(2, 4, ROWS, 256)
            return carry

        lax.fori_loop(0, 4, tile, 0)
        links.send(("core", s, k), parts.at[s, k, 1 - core], from_core.at[s, k], core_peer)

    def z_scatter(s, k):
        links.recv(("core", s, k), from_core.at[s, k])
        own = parts[s, k, core].astype(F32) + from_core[s, k].astype(F32)
        sums[s, k] = own.astype(BF)
        direct_start(
            links, ("zs", s, k), ring_z, lambda q: sums.at[s, k, q], lambda q: zgot.at[s, k, q]
        )

    def z_sum(s, k):
        links.recv(("zs", s, k), zgot.at[s, k, pl.ds(0, 3)])
        total = sums[s, k, z].astype(F32)
        for shift in (1, 2, 3):
            total += zgot[s, k, ring_z.at(shift)].astype(F32)
        return total

    def to_core(s, k, buf, shift):
        block = buf.at[k, core, ring_z.at(shift)]
        links.send(("zc", s, k), block, block, core_peer)

    def z_gather(s, k, buf):
        own = buf.at[k, core, z]
        direct_start(links, ("zg", s, k), ring_z, lambda q: own, lambda q: buf.at[k, core, q])
        to_core(s, k, buf, 0)

    def z_pass(s, k, buf):
        links.recv(("zg", s, k), buf.at[k, core, pl.ds(0, 3)])
        for shift in (1, 2, 3):
            to_core(s, k, buf, shift)

    def z_finish(s, k, buf):
        links.recv(("zc", s, k), buf.at[k, 1 - core])

    def encode(k):
        links.recv(("b2", k), got0.at[k, pl.ds(0, 3)])
        links.recv(("b3", k), got1.at[k, pl.ds(0, 3)])
        product(0, k, bank_chunk(k), enc)

    def latents(k):
        pre = z_sum(0, k) + bias_ref[...][None, :]
        soft = jnp.maximum(pre, 0.0) + jnp.log1p(jnp.exp(-jnp.abs(pre)))
        lat[k, core, z] = soft.astype(BF)
        slope[k] = jax.nn.sigmoid(pre)
        z_gather(0, k, lat)

    def decode(k):
        z_finish(0, k, lat)
        rows = lat[k].reshape(128, -1)
        over = (((1,), (1,)), ((), ()))
        out = lax.dot_general(rows, dec[:F0], over, preferred_element_type=F32)
        rp0[k] = out.astype(BF).reshape(4, 2, ROWS, F0)
        direct_start(links, ("xs", k), ring_x, lambda q: first(rp0, k, q), lambda q: got0.at[k, q])
        out = lax.dot_general(rows, dec[F0:], over, preferred_element_type=F32)
        rp1[k] = out.astype(BF).reshape(2, 2, 2, ROWS, features - F0)
        direct_start(links, ("ys", k), ring_y, lambda q: other(rp1, k, q), lambda q: got1.at[k, q])

    def recon_second(k):
        for tag, ring, own, got, s, d, next_ring in (
            ("x", ring_x, first(rp0, k, x), got0, s0, d0, ring_y),
            ("y", ring_y, other(rp1, k, y), got1, s1, d1, ring_x),
        ):
            links.recv((tag + "s", k), got.at[k, pl.ds(0, 3)])
            total = own[...].astype(F32)
            for shift in (1, 2, 3):
                total += got[k, ring.at(shift)].astype(F32)
            s[k] = total.astype(BF)
            direct_start(links, (tag + "t", k), next_ring, lambda q: s.at[k], lambda q: d.at[k, q])

    def recon_third(k):
        for tag, ring, s, d, t, e in (("xt", ring_y, s0, d0, q0, e0), ("yt", ring_x, s1, d1, q1, e1)):
            links.recv((tag, k), d.at[k, pl.ds(0, 3)])
            total = s[k].astype(F32)
            for shift in (1, 2, 3):
                total += d[k, ring.at(shift)].astype(F32)
            t[k] = total.astype(BF)
            links.send((tag + "z", k), t.at[k], e.at[k], zl_peer)

    def residual(k):
        j = 2 * lax.rem(y + k % 2, 2) + y // 2
        for tag, at, t, e, inputs, out, rows in (
            ("xt", pl.ds(0, F0), q0, e0, bank_first(k, x), first(rs0, k, x), bank_rows(k, 2 * x, 32)),
            ("yt", pl.ds(F0, features - F0), q1, e1, bank_other(k, y), other(rs1, k, y), bank_rows(k, j, 32, 4)),
        ):
            links.recv((tag + "z", k), e.at[k])
            weight = counts(rows) * scale
            for b in (0, 1):
                recon = t[k, b].astype(F32) + e[k, b].astype(F32) + dbias_ref[at][None, :]
                value = recon - inputs[b].astype(F32)
                out[b] = (value * weight[b * ROWS : (b + 1) * ROWS]).astype(BF)
        direct_start(links, ("r2", k), ring_x, lambda q: first(rs0, k, x), lambda q: first(rs0, k, q))
        direct_start(links, ("r3", k), ring_y, lambda q: other(rs1, k, y), lambda q: other(rs1, k, q))

    def resid_chunk(k):
        return rs0[k].reshape(128, F0), rs1[k].reshape(128, features - F0)

    def backward(k):
        links.recv(("r2", k), got0.at[k, pl.ds(0, 3)])
        links.recv(("r3", k), got1.at[k, pl.ds(0, 3)])
        product(1, k, resid_chunk(k), dec)

    def latent_gradient(k):
        weight = counts(bank_rows(k, core * 4 + z, ROWS))
        total_norm = norms_ref[0:1] + norms_ref[1:2] + norms_ref[2:3]
        grad = z_sum(1, k) + weight * (PENALTY * scale * total_norm)
        pg[k, core, z] = (grad * slope[k]).astype(BF)
        z_gather(1, k, pg)

    def bank_send():
        bank_copy.wait()
        blk0[zl] = bank_ref[:, :F0]
        blk1[zl] = bank_ref[:, F0:]
        links.send(("bz0",), blk0.at[zl], blk0.at[zl], zl_peer)
        links.send(("bz1",), blk1.at[zl], blk1.at[zl], zl_peer)

    def bank_recv():
        links.recv(("bz0",), blk0.at[1 - zl])
        links.recv(("bz1",), blk1.at[1 - zl])
        for low in (0, 1):
            own0 = bk0.at[low, x, y // 2, lax.rem(y, 2)]
            own1 = bk1.at[low, x // 2, lax.rem(x, 2), y]
            own0[...] = blk0[low]
            own1[...] = blk1[low]
            direct_start(
                links, ("b0", low), ring_y, lambda q: own0, lambda q: bk0.at[low, x, q // 2, lax.rem(q, 2)]
            )
            direct_start(
                links, ("b1", low), ring_x, lambda q: own1, lambda q: bk1.at[low, q // 2, lax.rem(q, 2), y]
            )

    def bank_second(low):
        links.recv(("b0", low), e0.at[pl.ds(0, 3), 0])
        links.recv(("b1", low), e1.at[pl.ds(0, 3), 0])
        bank_spread(2 * low)
        bank_spread(2 * low + 1)

    def squares_send():
        for copy in (*small_copies, dec_copy):
            copy.wait()
        row = lax.broadcasted_iota(jnp.int32, (8, features), 0)
        column = lax.broadcasted_iota(jnp.int32, (8, features), 1) + layer * features
        owner = jnp.where((column >= row * D) & (column < (row + 1) * D), 1.0, 0.0).astype(BF)

        def square(n, carry):
            at = pl.ds(pl.multiple_of(n * 256, 256), 256)
            wide = dec[:, at].astype(F32)
            wide = wide * wide
            high = wide.astype(BF)
            low = (wide - high.astype(F32)).astype(BF)
            total = jnp.dot(owner, high, preferred_element_type=F32)
            total += jnp.dot(owner, low, preferred_element_type=F32)
            sq_part[:, at] = total
            return carry

        lax.fori_loop(0, 4, square, 0)
        links.send(("sqc",), sq_part, sq_core, core_peer)

    def squares_second():
        links.recv(("sqc",), sq_core)
        sq_chip[...] = sq_part[...] + sq_core[...]
        direct_start(links, ("sqz",), ring_z, lambda q: sq_chip, lambda q: sq_z.at[q])

    def squares_sum():
        links.recv(("sqz",), sq_z.at[pl.ds(0, 3)])
        squares = sq_chip[...]
        for shift in (1, 2, 3):
            squares += sq_z[ring_z.at(shift)]
        norms_ref[...] = jnp.sqrt(squares + 1e-6)

    def copy_out(i, src, dst):
        copy = pltpu.make_async_copy(src, dst, local_sems.at[i])
        copy.start()
        outgoing.append(copy)

    def coefficients():
        colsum = jnp.zeros((1, lat.shape[-1]), F32)
        for k in range(CHUNKS):
            weight = counts(bank_rows(k, 0, 128))
            colsum += jnp.sum(lat[k].reshape(128, -1).astype(F32) * weight, axis=0, keepdims=True)
        coef_ref[...] = (PENALTY * scale * colsum) / norms_ref[...]

    def turn(buf, chunk, k):
        at = pl.ds(128 * k, 128)
        b0, b1 = chunk(k)
        buf[:F0, at] = b0.T
        buf[F0:, at] = b1.T

    def decoder_gradient(first, last):
        feature = layer * features + lax.broadcasted_iota(jnp.int32, (features, 1), 0)

        def tile(n, carry):
            at = pl.ds(pl.multiple_of(n * 256, 256), 256)
            rows = lat[:, :, :, :, at].reshape(512, 256)
            out = jnp.dot(resid_turned[...], rows, preferred_element_type=F32)
            spread = jnp.where(
                feature < D, coef_ref[0:1, at], jnp.where(feature < 2 * D, coef_ref[1:2, at], coef_ref[2:3, at])
            )
            dgrad[:, at] = (out + spread * dec[:, at].astype(F32)).astype(BF)
            return carry

        lax.fori_loop(first, last, tile, 0)

    outgoing = []
    chunk_steps = (
        (0.0, encode),
        (1.8, lambda k: z_scatter(0, k)),
        (8.0, latents),
        (14.3, lambda k: z_pass(0, k, lat)),
        (15.5, decode),
        (20.5, recon_second),
        (25.5, recon_third),
        (30.0, residual),
        (35.0, backward),
        (37.0, lambda k: z_scatter(1, k)),
        (43.0, latent_gradient),
        (49.5, lambda k: z_pass(1, k, pg)),
        (50.5, lambda k: z_finish(1, k, pg)),
    )
    once = (
        (-8.0, bank_send),
        (-7.0, bank_recv),
        (-6.0, squares_send),
        (-5.0, lambda: bank_second(0)),
        (-4.0, squares_second),
        (-3.0, lambda: bank_second(1)),
        (-2.0, enc_copy.wait),
        (9.0, squares_sum),
        (3 * LAG + 1.7, lambda: turn(turned, bank_chunk, 0)),
        (3 * LAG + 1.71, lambda: turn(turned, bank_chunk, 1)),
        (3 * LAG + 1.72, lambda: turn(turned, bank_chunk, 2)),
        (3 * LAG + 1.73, lambda: turn(turned, bank_chunk, 3)),
        (3 * LAG + 1.74, lambda: copy_out(2, turned, turned_out)),
        (3 * LAG + 16.0, coefficients),
        (3 * LAG + 36.5, lambda: turn(resid_turned, resid_chunk, 0)),
        (3 * LAG + 36.6, lambda: turn(resid_turned, resid_chunk, 1)),
        (3 * LAG + 37.1, lambda: turn(resid_turned, resid_chunk, 2)),
        (3 * LAG + 37.2, lambda: turn(resid_turned, resid_chunk, 3)),
        (3 * LAG + 37.3, lambda: decoder_gradient(0, 2)),
        (3 * LAG + 43.1, lambda: decoder_gradient(2, 4)),
        (3 * LAG + 43.2, lambda: copy_out(3, dgrad, dgrad_out)),
        (3 * LAG + 51.0, lambda: copy_out(4, pg, pg_out)),
    )
    timed = [(at, step, ()) for at, step in once]
    for k in range(CHUNKS):
        timed += [(at + LAG * k, step, (k,)) for at, step in chunk_steps]
    steps = [(step, *given) for at, step, given in sorted(timed, key=lambda entry: entry[0])]
    for step, *given in steps:
        step(*given)
    for family, view in (
        ("bz0", blk0.at[0]),
        ("bz1", blk1.at[0]),
        ("b0", e0.at[pl.ds(0, 3)]),
        ("b1", e1.at[pl.ds(0, 3)]),
        ("b2", got0.at[:, pl.ds(0, 3)]),
        ("b3", got1.at[:, pl.ds(0, 3)]),
        ("sqc", sq_part),
        ("sqz", sq_z.at[pl.ds(0, 3)]),
        ("core", sums),
        ("zs", zgot.at[:, :, pl.ds(0, 3)]),
        ("zg", zgot.at[:, :, pl.ds(0, 3)]),
        ("zc", sums),
        ("xs", got0.at[:, pl.ds(0, 3)]),
        ("ys", got1.at[:, pl.ds(0, 3)]),
        ("xt", got0.at[:, pl.ds(0, 3)]),
        ("yt", got1.at[:, pl.ds(0, 3)]),
        ("xtz", e0),
        ("ytz", e1),
        ("r2", got0.at[:, pl.ds(0, 3)]),
        ("r3", got1.at[:, pl.ds(0, 3)]),
    ):
        links.sent(family, view)
    for copy in outgoing:
        copy.wait()


def shards(ids, bank, enc_weight, enc_bias, dec_weight, dec_bias):
    tokens = ids.shape[0]
    features, lats = enc_weight.shape
    dec = dec_weight.T
    f1 = features - F0
    scale = 1.0 / math.sqrt(tokens)
    k = CHUNKS
    operands = (ids, bank, enc_bias, dec_bias, enc_weight, dec)
    messages = 80
    turned, dgrad, pg = pl.pallas_call(
        functools.partial(kernel, scale),
        out_shape=[
            jax.ShapeDtypeStruct((features, k * 128), BF),
            jax.ShapeDtypeStruct((features, lats), BF),
            jax.ShapeDtypeStruct((k, 2, 4, ROWS, lats), BF),
        ],
        in_specs=[pl.BlockSpec(memory_space=pl.ANY)] * 6,
        out_specs=[pl.BlockSpec(memory_space=pl.ANY)] * 3,
        scratch_shapes=[
            pltpu.VMEM(ids.shape, jnp.int32),
            pltpu.VMEM(bank.shape, BF),
            pltpu.VMEM(enc_bias.shape, F32),
            pltpu.VMEM(dec_bias.shape, F32),
            pltpu.VMEM((features, lats), BF),
            pltpu.VMEM((features, lats), BF),
            pltpu.VMEM((2, ROWS, F0), BF),
            pltpu.VMEM((2, ROWS, f1), BF),
            pltpu.VMEM((2, 4, 2, 2, ROWS, F0), BF),
            pltpu.VMEM((2, 2, 2, 4, ROWS, f1), BF),
            pltpu.VMEM((2, k, 2, 4, ROWS, lats), BF),
            pltpu.VMEM((2, k, 4, ROWS, lats), BF),
            pltpu.VMEM((2, k, 4, ROWS, lats), BF),
            pltpu.VMEM((2, k, 4, ROWS, lats), BF),
            pltpu.VMEM((k, 2, 4, ROWS, lats), BF),
            pltpu.VMEM((k, 2, 4, ROWS, lats), BF),
            pltpu.VMEM((k, ROWS, lats), F32),
            pltpu.VMEM((k, 4, 2, ROWS, F0), BF),
            pltpu.VMEM((k, 2, 2, 2, ROWS, f1), BF),
            pltpu.VMEM((k, 4, 2, ROWS, F0), BF),
            pltpu.VMEM((k, 4, 2, ROWS, f1), BF),
            pltpu.VMEM((k, 2, ROWS, F0), BF),
            pltpu.VMEM((k, 2, ROWS, f1), BF),
            pltpu.VMEM((k, 4, 2, ROWS, F0), BF),
            pltpu.VMEM((k, 4, 2, ROWS, f1), BF),
            pltpu.VMEM((k, 2, ROWS, F0), BF),
            pltpu.VMEM((k, 2, ROWS, f1), BF),
            pltpu.VMEM((k, 2, ROWS, F0), BF),
            pltpu.VMEM((k, 2, ROWS, f1), BF),
            pltpu.VMEM((k, 4, 2, ROWS, F0), BF),
            pltpu.VMEM((k, 2, 2, 2, ROWS, f1), BF),
            pltpu.VMEM((8, lats), F32),
            pltpu.VMEM((8, lats), F32),
            pltpu.VMEM((8, lats), F32),
            pltpu.VMEM((4, 8, lats), F32),
            pltpu.VMEM((8, lats), F32),
            pltpu.VMEM((8, lats), F32),
            pltpu.VMEM((features, k * 128), BF),
            pltpu.VMEM((features, k * 128), BF),
            pltpu.VMEM((features, lats), BF),
            pltpu.SemaphoreType.DMA((20,)),
            pltpu.SemaphoreType.DMA((messages,)),
            pltpu.SemaphoreType.DMA((9,)),
        ],
        compiler_params=pltpu.CompilerParams(
            collective_id=0, has_side_effects=True, vmem_limit_bytes=40 * 2**20
        ),
        name="crosscoder_step",
    )(*(pltpu.with_memory_space_constraint(a, pltpu.HBM) for a in operands))

    grad_encoder, grad_decoder = gradients(turned, pg.reshape(-1, lats), dgrad)
    return grad_encoder, grad_decoder.T


def gradients_kernel(turned, pg, dgrad, enc_grad, dec_grad, product, sems):
    copies = [pltpu.make_async_copy(dgrad, dec_grad, sems.at[0])]
    copies[0].start()
    pieces, size = product.shape[:2]
    for n in range(pieces):
        rows = pl.ds(n * size, size)
        product[n] = jnp.dot(turned[rows], pg[...], preferred_element_type=F32).astype(BF)
        copies.append(pltpu.make_async_copy(product.at[n], enc_grad.at[rows], sems.at[n + 1]))
        copies[-1].start()
    for copy in copies:
        copy.wait()


def gradients(turned, pg, dgrad):
    features, lats = dgrad.shape
    pieces = 3
    vmem = pl.BlockSpec(memory_space=pltpu.VMEM)
    memory = pl.BlockSpec(memory_space=pl.ANY)
    return pl.pallas_call(
        gradients_kernel,
        out_shape=[jax.ShapeDtypeStruct(dgrad.shape, BF)] * 2,
        in_specs=[vmem, vmem, memory],
        out_specs=[memory, memory],
        scratch_shapes=[
            pltpu.VMEM((pieces, features // pieces, lats), BF),
            pltpu.SemaphoreType.DMA((pieces + 1,)),
        ],
        compiler_params=pltpu.CompilerParams(vmem_limit_bytes=24 * 2**20),
        name="gradients",
    )(turned, pg, dgrad)


def solution(mesh):
    in_specs = (
        P(),
        P("latent", "layer"),
        P("layer", "latent"),
        P("latent"),
        P("latent", "layer"),
        P("layer"),
    )
    out_specs = (P("layer", "latent"), P("latent", "layer"))
    return jax.shard_map(shards, mesh=mesh, in_specs=in_specs, out_specs=out_specs, check_vma=False)
```

time: 661 us -> 102 us (0.15)
  waiting for transfers between devices: 585 us -> 0 us
  Pallas kernels: 0 us -> 101 us
  matrix products: 33.3 us -> 0 us
  blocking collectives: 15.8 us -> 0 us
  between operations: 13.9 us -> 0.64 us
  local copies, waits for them, and re-layouts: 8.2 us -> 0 us
    psum x3 -> x0, waiting for transfers between devices: 447 us -> none  [the longest x1 265 us: shards(): lax.psum(recon_part.astype(jnp.bfloat16), 'latent').astype(jnp.float32)]
    all_gather x1 -> x0, waiting for transfers between devices: 138 us -> none  [shards(): stored = lax.all_gather(bank, 'latent', axis=0, tiled=True)]
    pallas_call x0 -> x2, Pallas kernels: none -> 101 us  [the longest x1 98.4 us: shards(): pl.pallas_call(functools.partial(kernel, scale), out_shape=[jax.ShapeDtyp...]
    dot_general x7 -> x0, matrix products: 33.3 us -> none  [the longest x1 5.52 us: shards(): lax.dot_general(resid_grad, dec_weight, (((1,), (1,)), ((), ())), preferr...]
    psum x1 -> x0, blocking collectives: 15.8 us -> none  [shards(): lax.psum(square_part.astype(jnp.bfloat16), 'layer').astype(jnp.float32)]
    gather x2 -> x0, local copies, waits for them, and re-layouts: 8.18 us -> none  [shards(): inputs = jnp.take(stored, ids, axis=0)]
  transfers between devices with their start and end apart: 4 -> 0, of which waited for: 4 -> 0; matrix products, arithmetic and copies ran while one was open for 3% -> 0% of each run, Pallas kernels for 0% -> 0%
where the time goes in v4:
time: 102 us
  Pallas kernels  101 us (99%)
    pallas_call x1, Pallas kernels, shards(): pl.pallas_call(functools.partial(kernel, scale), out_shape=[jax.ShapeDtyp...  98.4 us
    pallas_call x1, Pallas kernels, gradients(): pl.pallas_call(gradients_kernel, out_shape=[jax.ShapeDtypeStruct(dgrad.sh...  2.56 us

profile of v4, /device:TPU:1, one launch (start us, length us, event | category | flops | bytes accessed | tf_op | source)
XLA Modules:
  0.0 101.6 jit_solution(8441626177412813912)
XLA Ops:
  0.6 98.4 %crosscoder_step.1 = (bf16[1344,512]{1,0:T(8,128)(2,1)S(1)}, bf16[1344,1024]{1,0:T(8,128)(2,1)S(1)}, bf16[4,2,4,16,1024]{4,3,2,1,0:T(8,128)(2,1)S(1)}) custom-call(s32[512]{0:T(512)} %ids_hbm.1, bf16[16,1344]{1,0:T(8,128)(2,1)} %bank_hbm.1, f32[1024]{0:T(1024)} %bias_hbm.1, f32[1344]{0:T(1024)} %dbias_hbm.1, bf16[1344,1024]{1,0:T(8,128)(2,1)} %enc_hbm.1, ...), custom_call_target="tpu_custom_call" | custom-call | tf_op jit(solution)/shard_map/crosscoder_step/pallas_call | solution.py:434
  99.0 2.6 %gradients.1 = (bf16[1344,1024]{1,0:T(8,128)(2,1)}, bf16[1344,1024]{1,0:T(8,128)(2,1)}) custom-call(bf16[1344,512]{1,0:T(8,128)(2,1)S(1)} %get-tuple-element.7.turned, bf16[512,1024]{1,0:T(8,128)(2,1)S(1)} %bitcast.3, bf16[1344,1024]{1,0:T(8,128)(2,1)S(1)} %get-tuple-element.9.dgrad), custom_call_target="tpu_custom_call" | custom-call | tf_op jit(solution)/shard_map/gradients/pallas_call | solution.py:516

commit v5 on v4

--- a/solution.py
+++ b/solution.py
@@ -14,7 +14,11 @@
 ROWS = 16
 F0 = 640
 CHUNKS = 4
-LAG = 4.5
+ORDER = (
+    0, 1, 0, 0, 3, 2, 1, 1, 4, 0, 1, 2, 3, 3, 0, 0, 2, 1, 1, 3, 0,
+    2, 5, 3, 1, 0, 3, 0, 1, 2, 3, 2, 0, 1, 0, 3, 2, 6, 1, 3, 1, 2,
+    0, 7, 3, 2, 3, 1, 2, 2, 0, 8, 1, 3, 9, 2, 10, 3, 1, 3, 0, 2, 2,
+)
 MESH = pl.DeviceIdType.MESH
 BF = jnp.bfloat16
 F32 = jnp.float32
@@ -88,9 +92,9 @@
 
     dec_copy = pltpu.make_async_copy(dec_hbm, dec, local_sems.at[0])
     enc_copy = pltpu.make_async_copy(enc_hbm, enc, local_sems.at[1])
-    bank_copy = pltpu.make_async_copy(bank_hbm, bank_ref, local_sems.at[5])
+    bank_copy = pltpu.make_async_copy(bank_hbm, bank_ref, local_sems.at[8])
     small_copies = [
-        pltpu.make_async_copy(src, dst, local_sems.at[6 + i])
+        pltpu.make_async_copy(src, dst, local_sems.at[9 + i])
         for i, (src, dst) in enumerate(((ids_hbm, ids_ref), (bias_hbm, bias_ref), (dbias_hbm, dbias_ref)))
     ]
     for copy in (bank_copy, *small_copies, dec_copy, enc_copy):
@@ -146,7 +150,7 @@
             parts[s, k, :, :, :, at] = out.astype(BF).reshape(2, 4, ROWS, 256)
             return carry
 
-        lax.fori_loop(0, 4, tile, 0)
+        lax.fori_loop(0, 4, tile, 0, unroll=True)
         links.send(("core", s, k), parts.at[s, k, 1 - core], from_core.at[s, k], core_peer)
 
     def z_scatter(s, k):
@@ -277,11 +281,18 @@
                 links, ("b1", low), ring_x, lambda q: own1, lambda q: bk1.at[low, q // 2, lax.rem(q, 2), y]
             )
 
-    def bank_second(low):
-        links.recv(("b0", low), e0.at[pl.ds(0, 3), 0])
-        links.recv(("b1", low), e1.at[pl.ds(0, 3), 0])
-        bank_spread(2 * low)
-        bank_spread(2 * low + 1)
+    first_done = []
+
+    def bank_second(k):
+        if k // 2 not in first_done:
+            first_done.append(k // 2)
+            links.recv(("b0", k // 2), e0.at[pl.ds(0, 3), 0])
+            links.recv(("b1", k // 2), e1.at[pl.ds(0, 3), 0])
+        bank_spread(k)
+        if k == 1:
+            squares_send()
+            squares_second()
+            enc_copy.wait()
 
     def squares_send():
         for copy in (*small_copies, dec_copy):
@@ -301,7 +312,7 @@
             sq_part[:, at] = total
             return carry
 
-        lax.fori_loop(0, 4, square, 0)
+        lax.fori_loop(0, 4, square, 0, unroll=True)
         links.send(("sqc",), sq_part, sq_core, core_peer)
 
     def squares_second():
@@ -350,49 +361,54 @@
         lax.fori_loop(first, last, tile, 0)
 
     outgoing = []
+    def finish_chunk(k):
+        z_finish(1, k, pg)
+        copy_out(4 + k, pg.at[k], pg_out.at[k])
+
     chunk_steps = (
-        (0.0, encode),
-        (1.8, lambda k: z_scatter(0, k)),
-        (8.0, latents),
-        (14.3, lambda k: z_pass(0, k, lat)),
-        (15.5, decode),
-        (20.5, recon_second),
-        (25.5, recon_third),
-        (30.0, residual),
-        (35.0, backward),
-        (37.0, lambda k: z_scatter(1, k)),
-        (43.0, latent_gradient),
-        (49.5, lambda k: z_pass(1, k, pg)),
-        (50.5, lambda k: z_finish(1, k, pg)),
+        bank_second,
+        encode,
+        lambda k: z_scatter(0, k),
+        latents,
+        lambda k: z_pass(0, k, lat),
+        decode,
+        recon_second,
+        recon_third,
+        residual,
+        backward,
+        lambda k: z_scatter(1, k),
+        latent_gradient,
+        lambda k: z_pass(1, k, pg),
+        finish_chunk,
     )
+
+    def turn_bank(first, last):
+        for k in (first, last):
+            turn(turned, bank_chunk, k)
+        if last == 3:
+            copy_out(2, turned, turned_out)
+
+    def turn_resid(first, last):
+        for k in (first, last):
+            turn(resid_turned, resid_chunk, k)
+
+    def finish_decoder():
+        decoder_gradient(2, 4)
+        copy_out(3, dgrad, dgrad_out)
+
     once = (
-        (-8.0, bank_send),
-        (-7.0, bank_recv),
-        (-6.0, squares_send),
-        (-5.0, lambda: bank_second(0)),
-        (-4.0, squares_second),
-        (-3.0, lambda: bank_second(1)),
-        (-2.0, enc_copy.wait),
-        (9.0, squares_sum),
-        (3 * LAG + 1.7, lambda: turn(turned, bank_chunk, 0)),
-        (3 * LAG + 1.71, lambda: turn(turned, bank_chunk, 1)),
-        (3 * LAG + 1.72, lambda: turn(turned, bank_chunk, 2)),
-        (3 * LAG + 1.73, lambda: turn(turned, bank_chunk, 3)),
-        (3 * LAG + 1.74, lambda: copy_out(2, turned, turned_out)),
-        (3 * LAG + 16.0, coefficients),
-        (3 * LAG + 36.5, lambda: turn(resid_turned, resid_chunk, 0)),
-        (3 * LAG + 36.6, lambda: turn(resid_turned, resid_chunk, 1)),
-        (3 * LAG + 37.1, lambda: turn(resid_turned, resid_chunk, 2)),
-        (3 * LAG + 37.2, lambda: turn(resid_turned, resid_chunk, 3)),
-        (3 * LAG + 37.3, lambda: decoder_gradient(0, 2)),
-        (3 * LAG + 43.1, lambda: decoder_gradient(2, 4)),
-        (3 * LAG + 43.2, lambda: copy_out(3, dgrad, dgrad_out)),
-        (3 * LAG + 51.0, lambda: copy_out(4, pg, pg_out)),
+        lambda: (squares_sum(), turn_bank(0, 1)),
+        lambda: turn_bank(2, 3),
+        coefficients,
+        lambda: turn_resid(0, 1),
+        lambda: turn_resid(2, 3),
+        lambda: decoder_gradient(0, 2),
+        finish_decoder,
     )
-    timed = [(at, step, ()) for at, step in once]
-    for k in range(CHUNKS):
-        timed += [(at + LAG * k, step, (k,)) for at, step in chunk_steps]
-    steps = [(step, *given) for at, step, given in sorted(timed, key=lambda entry: entry[0])]
+    steps = [(bank_send,), (bank_recv,)]
+    left = [iter(chunk_steps) for k in range(CHUNKS)]
+    for k in ORDER:
+        steps.append((next(left[k]), k) if k < CHUNKS else (once[k - CHUNKS],))
     for step, *given in steps:
         step(*given)
     for family, view in (
@@ -483,7 +499,7 @@
             pltpu.VMEM((features, lats), BF),
             pltpu.SemaphoreType.DMA((20,)),
             pltpu.SemaphoreType.DMA((messages,)),
-            pltpu.SemaphoreType.DMA((9,)),
+            pltpu.SemaphoreType.DMA((12,)),
         ],
         compiler_params=pltpu.CompilerParams(
             collective_id=0, has_side_effects=True, vmem_limit_bytes=40 * 2**20

time: 102 us -> 97.6 us (0.957)
  Pallas kernels: 101 us -> 96.7 us
    pallas_call x1, Pallas kernels: 98.4 us -> 94.1 us  [shards(): pl.pallas_call(functools.partial(kernel, scale), out_shape=[jax.ShapeDtyp...]
where the time goes in v5:
time: 97.6 us; the launch traced here: 97.5 us
  Pallas kernels  96.7 us (99%)
    pallas_call x1, Pallas kernels, shards(): pl.pallas_call(functools.partial(kernel, scale), out_shape=[jax.ShapeDtyp...  94.1 us
    pallas_call x1, Pallas kernels, gradients(): pl.pallas_call(gradients_kernel, out_shape=[jax.ShapeDtypeStruct(dgrad.sh...  2.56 us

profile of v5, /device:TPU:1, one launch (start us, length us, event | category | flops | bytes accessed | tf_op | source)
XLA Modules:
  0.0 97.5 jit_solution(6875512651771840321)
XLA Ops:
  0.6 94.1 %crosscoder_step.1 = (bf16[1344,512]{1,0:T(8,128)(2,1)S(1)}, bf16[1344,1024]{1,0:T(8,128)(2,1)S(1)}, bf16[4,2,4,16,1024]{4,3,2,1,0:T(8,128)(2,1)S(1)}) custom-call(s32[512]{0:T(512)} %ids_hbm.1, bf16[16,1344]{1,0:T(8,128)(2,1)} %bank_hbm.1, f32[1024]{0:T(1024)} %bias_hbm.1, f32[1344]{0:T(1024)} %dbias_hbm.1, bf16[1344,1024]{1,0:T(8,128)(2,1)} %enc_hbm.1, ...), custom_call_target="tpu_custom_call" | custom-call | tf_op jit(solution)/shard_map/crosscoder_step/pallas_call | solution.py:450
  94.8 2.6 %gradients.1 = (bf16[1344,1024]{1,0:T(8,128)(2,1)}, bf16[1344,1024]{1,0:T(8,128)(2,1)}) custom-call(bf16[1344,512]{1,0:T(8,128)(2,1)S(1)} %get-tuple-element.7.turned, bf16[512,1024]{1,0:T(8,128)(2,1)S(1)} %bitcast.3, bf16[1344,1024]{1,0:T(8,128)(2,1)S(1)} %get-tuple-element.9.dgrad), custom_call_target="tpu_custom_call" | custom-call | tf_op jit(solution)/shard_map/gradients/pallas_call | solution.py:532

commit v6 on v5

--- a/solution.py
+++ b/solution.py
@@ -15,9 +15,9 @@
 F0 = 640
 CHUNKS = 4
 ORDER = (
-    0, 1, 0, 0, 3, 2, 1, 1, 4, 0, 1, 2, 3, 3, 0, 0, 2, 1, 1, 3, 0,
-    2, 5, 3, 1, 0, 3, 0, 1, 2, 3, 2, 0, 1, 0, 3, 2, 6, 1, 3, 1, 2,
-    0, 7, 3, 2, 3, 1, 2, 2, 0, 8, 1, 3, 9, 2, 10, 3, 1, 3, 0, 2, 2,
+    0, 1, 2, 0, 3, 0, 1, 1, 2, 0, 1, 3, 3, 2, 4, 5, 0, 0, 1, 1, 3,
+    0, 2, 1, 0, 3, 3, 2, 0, 1, 2, 6, 3, 0, 2, 0, 3, 1, 2, 3, 0, 1,
+    2, 1, 3, 3, 2, 7, 8, 2, 9, 1, 0, 3, 2, 10, 1, 0, 3, 2, 1, 3, 2,
 )
 MESH = pl.DeviceIdType.MESH
 BF = jnp.bfloat16
@@ -317,7 +317,10 @@
 
     def squares_second():
         links.recv(("sqc",), sq_core)
-        sq_chip[...] = sq_part[...] + sq_core[...]
+        total = sq_part[...] + sq_core[...]
+        for l in range(LAYERS):
+            for g in range(8):
+                sq_chip[g : g + 1, 128 * l : 128 * l + 128] = total[l : l + 1, 128 * g : 128 * g + 128]
         direct_start(links, ("sqz",), ring_z, lambda q: sq_chip, lambda q: sq_z.at[q])
 
     def squares_sum():
@@ -325,7 +328,11 @@
         squares = sq_chip[...]
         for shift in (1, 2, 3):
             squares += sq_z[ring_z.at(shift)]
-        norms_ref[...] = jnp.sqrt(squares + 1e-6)
+        norms = jnp.sqrt(squares + 1e-6)
+        norms_ref[...] = jnp.ones(norms_ref.shape, F32)
+        for l in range(LAYERS):
+            for g in range(8):
+                norms_ref[l : l + 1, 128 * g : 128 * g + 128] = norms[g : g + 1, 128 * l : 128 * l + 128]
 
     def copy_out(i, src, dst):
         copy = pltpu.make_async_copy(src, dst, local_sems.at[i])
@@ -490,8 +497,8 @@
             pltpu.VMEM((k, 2, 2, 2, ROWS, f1), BF),
             pltpu.VMEM((8, lats), F32),
             pltpu.VMEM((8, lats), F32),
-            pltpu.VMEM((8, lats), F32),
-            pltpu.VMEM((4, 8, lats), F32),
+            pltpu.VMEM((8, 128 * LAYERS), F32),
+            pltpu.VMEM((4, 8, 128 * LAYERS), F32),
             pltpu.VMEM((8, lats), F32),
             pltpu.VMEM((8, lats), F32),
             pltpu.VMEM((features, k * 128), BF),

time: 97.6 us -> 95.7 us (0.981)
  Pallas kernels: 96.7 us -> 93.9 us
    pallas_call x1, Pallas kernels: 94.1 us -> 91.3 us  [shards(): pl.pallas_call(functools.partial(kernel, scale), out_shape=[jax.ShapeDtyp...]
where the time goes in v6:
time: 95.7 us; the launch traced here: 94.7 us
  Pallas kernels  93.9 us (98%)
    pallas_call x1, Pallas kernels, shards(): pl.pallas_call(functools.partial(kernel, scale), out_shape=[jax.ShapeDtyp...  91.3 us
    pallas_call x1, Pallas kernels, gradients(): pl.pallas_call(gradients_kernel, out_shape=[jax.ShapeDtypeStruct(dgrad.sh...  2.56 us

profile of v6, /device:TPU:1, one launch (start us, length us, event | category | flops | bytes accessed | tf_op | source)
XLA Modules:
  0.0 94.7 jit_solution(17888871049739568140)
XLA Ops:
  0.6 91.3 %crosscoder_step.1 = (bf16[1344,512]{1,0:T(8,128)(2,1)S(1)}, bf16[1344,1024]{1,0:T(8,128)(2,1)S(1)}, bf16[4,2,4,16,1024]{4,3,2,1,0:T(8,128)(2,1)S(1)}) custom-call(s32[512]{0:T(512)} %ids_hbm.1, bf16[16,1344]{1,0:T(8,128)(2,1)} %bank_hbm.1, f32[1024]{0:T(1024)} %bias_hbm.1, f32[1344]{0:T(1024)} %dbias_hbm.1, bf16[1344,1024]{1,0:T(8,128)(2,1)} %enc_hbm.1, ...), custom_call_target="tpu_custom_call" | custom-call | tf_op jit(solution)/shard_map/crosscoder_step/pallas_call | solution.py:457
  91.9 2.6 %gradients.1 = (bf16[1344,1024]{1,0:T(8,128)(2,1)}, bf16[1344,1024]{1,0:T(8,128)(2,1)}) custom-call(bf16[1344,512]{1,0:T(8,128)(2,1)S(1)} %get-tuple-element.7.turned, bf16[512,1024]{1,0:T(8,128)(2,1)S(1)} %bitcast.3, bf16[1344,1024]{1,0:T(8,128)(2,1)S(1)} %get-tuple-element.9.dgrad), custom_call_target="tpu_custom_call" | custom-call | tf_op jit(solution)/shard_map/gradients/pallas_call | solution.py:539
